TPU v7x, 512 devices: a whole 4x8x8 slice. The times are simulated.
512 devices in a mesh: dp: 8 (over y), seq: 16 (over z, core), head: 4 (over x).
Axes of the slice: x: 4, y: 8, z: 8, core: 2. Of those that a mesh axis runs over, the one named last changes fastest.
Arguments:
- enc_query: bfloat16 [8, 2048, 1536], P('dp', 'seq', 'head'), may hold values from -240 to 240
- enc_key: bfloat16 [8, 2048, 1536], P('dp', 'seq', 'head'), may hold values from -6 to 6
- enc_value: bfloat16 [8, 2048, 1536], P('dp', 'seq', 'head'), may hold values from -6 to 6
- keep_index: int32 [8, 1536], P('dp', 'seq'), may hold values from 0 to 127, as said below
- keep_count: int32 [8, 16], P('dp', 'seq'), may hold values from 32 to 96, as said below
- text_key: bfloat16 [8, 128, 1536], P('dp', None, 'head'), may hold values from -6 to 6
- text_value: bfloat16 [8, 128, 1536], P('dp', None, 'head'), may hold values from -6 to 6
- dec_query: bfloat16 [8, 2048, 1536], P('dp', 'seq', 'head'), may hold values from -240 to 240
- dec_key: bfloat16 [8, 2048, 1536], P('dp', 'seq', 'head'), may hold values from -6 to 6
- mask_value: bfloat16 [1536], P('head'), may hold values from -5 to 5
- norm_gain: bfloat16 [1536], P('head'), may hold values from 0.25 to 1.75
- target: bfloat16 [8, 2048, 1536], P('dp', 'seq', 'head'), may hold values from -6 to 6
- timesteps: int32 [8], P('dp'), may hold values from 0 to 999
Outputs:
- decoded: bfloat16 [8, 2048, 1536], P('dp', 'seq', 'head')
- total_loss: float32 [], replicated
Inputs may be any that keep to these rules, and one draw needn't show every extreme that they name: `keep_count`: each image has one block whose count is exactly 96. `keep_index`: in each block's 96 slots the first keep_count entries are strictly increasing, the rest are 0.
All inputs are finite; a program needn't handle non-finite values.
Results may differ from a plain program's by a relative error of at most 0.004.
Values may be sent and summed in bfloat16 or wider, within the bound.
No kernel may reach another device: no remote copies, remote signals or barrier semaphores. Data moves between devices by JAX's collectives and lax.ppermute only.
A program may use at most 64 MiB of HBM per device.

v0:
```python
import functools

import jax
import jax.numpy as jnp
from jax import lax
from jax.experimental import pallas as pl
from jax.experimental.pallas import tpu as pltpu
from jax.sharding import PartitionSpec as P

HEAD_DIM = 64
LANES = 128
DEAD = 1024.0
DEAD_EDGE = 512.0
MIB = 1024 * 1024


def params(mib=40):
    return pltpu.CompilerParams(vmem_limit_bytes=mib * MIB)


def vmem(count):
    return [pl.BlockSpec(memory_space=pltpu.VMEM)] * count


def one_hot_dot(table, rows):
    return lax.dot_general(
        table, rows, (((1,), (0,)), ((), ())), preferred_element_type=jnp.float32
    )


def pack_kernel(
    count_ref, index_hbm, eq_hbm, ek_hbm, ev_hbm, dq_hbm, dk_hbm, send_ref, *scratch
):
    *held, sems = scratch
    given = (index_hbm, eq_hbm, ek_hbm, ev_hbm, dq_hbm, dk_hbm)
    copies = [
        pltpu.make_async_copy(source, place, sems.at[number])
        for number, (source, place) in enumerate(zip(given, held))
    ]
    for copy in copies:
        copy.start()
    copies[0].wait()
    index_ref, eq_ref, ek_ref, ev_ref, dq_ref, dk_ref = held
    tokens, cols = eq_ref.shape[1:]
    slots = index_ref.shape[1]
    heads = cols // HEAD_DIM
    spare = tokens - slots
    total = count_ref[0, 0]
    index = jnp.broadcast_to(index_ref[...].astype(jnp.float32), (tokens, slots))
    index = jnp.transpose(index)
    token = lax.broadcasted_iota(jnp.int32, (slots, tokens), 1).astype(jnp.float32)
    slot = lax.broadcasted_iota(jnp.int32, (slots, tokens), 0)
    live = slot < total
    match_live = jnp.where(live & (token == index), 1.0, 0.0)
    match_fill = jnp.where(token == jnp.where(live, index, index[0:1, :]), 1.0, 0.0)
    kept = jnp.sum(match_live, axis=0, keepdims=True)
    kept_slot = jnp.sum(match_live * slot.astype(jnp.float32), axis=0, keepdims=True)
    row = lax.broadcasted_iota(jnp.int32, (tokens, tokens), 0)
    col = lax.broadcasted_iota(jnp.int32, (tokens, tokens), 1)
    before = jnp.where(row < col, 1.0, 0.0).astype(jnp.bfloat16)
    left = jnp.broadcast_to(1.0 - kept, (16, tokens)).astype(jnp.bfloat16)
    rank = one_hot_dot(left, before)[0:1, :]
    place = jnp.where(kept > 0.5, kept_slot, total.astype(jnp.float32) + rank)
    order = jnp.where(row.astype(jnp.float32) == place, 1.0, 0.0).astype(jnp.bfloat16)

    for copy in copies[1:]:
        copy.wait()
    scale = HEAD_DIM ** (-0.5)
    match_live = match_live.astype(jnp.bfloat16)
    match_fill = match_fill.astype(jnp.bfloat16)
    query = one_hot_dot(match_live, eq_ref[0]) * scale
    slot_wide = lax.broadcasted_iota(jnp.int32, (slots, cols), 0)
    query = jnp.where(slot_wide < total, query, DEAD)
    key = one_hot_dot(match_fill, ek_ref[0])
    value = one_hot_dot(match_live, ev_ref[0])
    dec_key = one_hot_dot(order, dk_ref[0])
    dec_query = dq_ref[0].astype(jnp.float32) * scale

    def low(block, head):
        tile = block[:, (head // 2) * LANES : (head // 2 + 1) * LANES]
        return tile if head % 2 == 0 else pltpu.roll(tile, HEAD_DIM, 1)

    def high(block, head):
        tile = block[:, (head // 2) * LANES : (head // 2 + 1) * LANES]
        return tile if head % 2 == 1 else pltpu.roll(tile, HEAD_DIM, 1)

    def join(first, second):
        lane = lax.broadcasted_iota(jnp.int32, first.shape, 1)
        return jnp.where(lane < HEAD_DIM, first, second).astype(jnp.bfloat16)

    for head in range(heads):
        kept_tile = join(low(value, head), high(key, head))
        query_high = high(query, head)
        dec_low = low(dec_key, head)
        dq_low = low(dec_query, head)
        dq_high = high(dec_query, head)
        send_ref[head, 0:slots, :] = kept_tile
        send_ref[head, slots : 2 * slots, :] = join(dec_low[0:slots], query_high)
        send_ref[head, 2 * slots : slots + tokens, :] = join(dec_low[slots:tokens], dq_high[0:spare])
        rest = slots // 2
        send_ref[head, slots + tokens : slots + tokens + rest, :] = join(
            dq_low[spare : spare + rest], dq_high[spare + rest : tokens]
        )


def put_scores(query, key_refs, place, peak):
    rows = query.shape[0]
    largest = None
    column = 0
    for key_ref in key_refs:
        keys = key_ref.shape[0]
        for first in range(0, keys, 2 * LANES):
            last = min(keys, first + 2 * LANES)
            part = lax.dot_general(
                query, key_ref[first:last, :], (((1,), (1,)), ((), ())), preferred_element_type=jnp.float32
            )
            place[0:rows, column : column + last - first] = part
            column += last - first
            for lane in range(0, last - first, LANES):
                tile = part[:, lane : lane + LANES]
                largest = tile if largest is None else jnp.maximum(largest, tile)
    peak[0:rows, :] = largest


def weigh(rows, place, peak, value_refs, earlier):
    top = jnp.max(peak[0:rows, :], axis=1, keepdims=True)
    sums = None
    if earlier is not None:
        earlier_sums, earlier_top = earlier
        top = jnp.maximum(top, earlier_top[:, 0:1])
        sums = earlier_sums * jnp.exp(earlier_top - top)
    column = 0
    for value_ref in value_refs:
        keys = value_ref.shape[0]
        weights = jnp.exp(place[0:rows, column : column + keys] - top).astype(jnp.bfloat16)
        column += keys
        part = lax.dot_general(
            weights, value_ref[...], (((1,), (0,)), ((), ())), preferred_element_type=jnp.float32
        )
        sums = part if sums is None else sums + part
    return top, sums


def run_jobs(jobs, buffers):
    def put(number):
        query, key_refs, _, _, _ = jobs[number]
        put_scores(query(), key_refs, *buffers[number % 2])

    put(0)
    for number, (query, _, value_refs, earlier, use) in enumerate(jobs):
        if number + 1 < len(jobs):
            put(number + 1)
        place, peak = buffers[number % 2]
        rows = query().shape[0]
        use(*weigh(rows, place, peak, value_refs, None if earlier is None else earlier()))


def lane_of(rows):
    return lax.broadcasted_iota(jnp.int32, (rows, LANES), 1)


def unpack(slots, tokens, got, block, first_key, first_dec, ek_ref, ev_ref, eq_ref, dk_ref):
    kept = got[0:slots, :]
    mixed = got[slots : 2 * slots, :].astype(jnp.float32)
    low = lane_of(slots) < HEAD_DIM
    base = first_key + block * slots
    ek_ref[base : base + slots, :] = kept
    ev_ref[base : base + slots, :] = jnp.where(
        low, kept.astype(jnp.float32), jnp.where(mixed < DEAD_EDGE, 1.0, 0.0)
    ).astype(jnp.bfloat16)
    eq_ref[block * slots : block * slots + slots, :] = jnp.where(low, 0.0, mixed).astype(jnp.bfloat16)
    base = first_dec + block * tokens
    dk_ref[base : base + tokens, :] = got[slots : slots + tokens, :]


def begin_kernel(
    slots,
    tokens,
    own_ref,
    text_key_ref,
    text_value_ref,
    mask_ref,
    ek_ref,
    ev_ref,
    eq_ref,
    dk_ref,
    dq_ref,
    sums_ref,
    top_ref,
    fill_ref,
    *places
):
    chips = own_ref.shape[0]
    cols = text_key_ref.shape[2]
    spare = tokens - slots
    rest = slots // 2
    head = jnp.minimum(lax.axis_index("seq") // 2, cols // HEAD_DIM - 1)
    odd = lax.rem(head, 2) == 1
    lanes = pl.ds(pl.multiple_of((head // 2) * LANES, LANES), LANES)

    def low_high(rows):
        turned = pltpu.roll(rows, HEAD_DIM, 1)
        return jnp.where(odd, turned, rows), jnp.where(odd, rows, turned)

    key_low, key_high = low_high(text_key_ref[0, :, lanes].astype(jnp.float32))
    value_low, _ = low_high(text_value_ref[0, :, lanes].astype(jnp.float32))
    mask_row = jnp.zeros((1, LANES), jnp.float32)
    whole = mask_ref[...].astype(jnp.float32).reshape(1, cols)
    for tile in range(cols // LANES):
        mask_row = jnp.where(head // 2 == tile, whole[:, tile * LANES : (tile + 1) * LANES], mask_row)
    mask_row, _ = low_high(jnp.broadcast_to(mask_row, (8, LANES)))
    low = lane_of(tokens) < HEAD_DIM
    fill_ref[...] = jnp.where(lane_of(8) < HEAD_DIM, mask_row, 1.0)
    ek_ref[0:tokens, :] = jnp.where(low, value_low, key_high).astype(jnp.bfloat16)
    ev_ref[0:tokens, :] = jnp.where(low, value_low, 1.0).astype(jnp.bfloat16)
    dk_ref[0:tokens, :] = key_low.astype(jnp.bfloat16)
    for block in range(chips):
        got = own_ref.at[block]
        unpack(slots, tokens, got, block, tokens, tokens, ek_ref, ev_ref, eq_ref, dk_ref)
        tail = got[2 * slots : slots + tokens, :].astype(jnp.float32)
        last = got[slots + tokens : slots + tokens + rest, :].astype(jnp.float32)
        base = block * tokens
        dq_ref[base : base + spare, :] = jnp.where(
            lane_of(spare) < HEAD_DIM, pltpu.roll(tail, HEAD_DIM, 1), 0.0
        ).astype(jnp.bfloat16)
        low_rest = lane_of(rest) < HEAD_DIM
        dq_ref[base + spare : base + spare + rest, :] = jnp.where(low_rest, last, 0.0).astype(jnp.bfloat16)
        dq_ref[base + spare + rest : base + tokens, :] = jnp.where(
            low_rest, pltpu.roll(last, HEAD_DIM, 1), 0.0
        ).astype(jnp.bfloat16)

    rows = chips // 2 * slots

    def job(tile):
        span = slice(tile * rows, (tile + 1) * rows)

        def use(top, sums):
            sums_ref[span, :] = sums
            top_ref[span, :] = jnp.broadcast_to(top, (rows, LANES))

        return (lambda: eq_ref[span, :], [ek_ref], [ev_ref], None, use)

    run_jobs([job(tile) for tile in range(2)], (places[0:2], places[2:4]))


def attend_kernel(
    slots,
    tokens,
    pair_ref,
    ek_ref,
    ev_ref,
    eq_ref,
    dk_ref,
    dq_ref,
    sums_ref,
    top_ref,
    fill_ref,
    out_ref,
    pair_ek_ref,
    pair_ev_ref,
    pair_eq_ref,
    pair_dk_ref,
    dv_ref,
    *places
):
    chips = pair_ref.shape[0]
    spare = tokens - slots
    for block in range(chips):
        unpack(
            slots, tokens, pair_ref.at[block], block, 0, 0, pair_ek_ref, pair_ev_ref, pair_eq_ref, pair_dk_ref
        )
    dv_ref[0:tokens, :] = ev_ref[0:tokens, :]
    mask_row = fill_ref[0:1, :]
    fill = jnp.broadcast_to(mask_row, (spare, LANES)).astype(jnp.bfloat16)
    group = chips // 2
    rows = group * slots

    def encode(tile, query_ref, first_block, key_refs, value_refs, earlier):
        span = slice(tile * rows, (tile + 1) * rows)

        def use(top, sums):
            found = sums / pltpu.roll(sums, HEAD_DIM, 1)
            for inner in range(group):
                mixed = query_ref[tile * rows + inner * slots : tile * rows + (inner + 1) * slots, :]
                live = pltpu.roll(mixed.astype(jnp.float32), HEAD_DIM, 1) < DEAD_EDGE
                base = tokens + (first_block + tile * group + inner) * tokens
                dv_ref[base : base + slots, :] = jnp.where(
                    (lane_of(slots) < HEAD_DIM) & live, found[inner * slots : (inner + 1) * slots, :], mask_row
                ).astype(jnp.bfloat16)
                dv_ref[base + slots : base + tokens, :] = fill

        before = (lambda: (sums_ref[span, :], top_ref[span, :])) if earlier else None
        return (lambda: query_ref[span, :], key_refs, value_refs, before, use)

    dec_group = 2
    dec_rows = dec_group * tokens
    half = tokens // 2

    def decode(tile):
        def use(top, sums):
            found = sums / pltpu.roll(sums, HEAD_DIM, 1)
            for inner in range(dec_group):
                first = inner * tokens
                out_ref[tile * dec_group + inner] = jnp.where(
                    lane_of(half) < HEAD_DIM,
                    found[first : first + half],
                    pltpu.roll(found[first + half : first + tokens], HEAD_DIM, 1),
                ).astype(jnp.bfloat16)

        span = slice(tile * dec_rows, (tile + 1) * dec_rows)
        return (lambda: dq_ref[span, :], [dk_ref, pair_dk_ref], [dv_ref], None, use)

    jobs = [encode(tile, eq_ref, 0, [pair_ek_ref], [pair_ev_ref], True) for tile in range(2)]
    jobs += [
        encode(tile, pair_eq_ref, chips, [ek_ref, pair_ek_ref], [ev_ref, pair_ev_ref], False) for tile in range(2)
    ]
    jobs += [decode(tile) for tile in range(chips // dec_group)]
    run_jobs(jobs, (places[0:2], places[2:4]))


def sums_kernel(got_ref, gain_ref, target_ref, weight_ref, att_ref, sums_ref):
    tokens, cols = att_ref.shape
    half = tokens // 2
    low = lax.broadcasted_iota(jnp.int32, (half, LANES), 1) < HEAD_DIM
    for tile in range(cols // LANES):
        even = got_ref[2 * tile].astype(jnp.float32)
        odd = got_ref[2 * tile + 1].astype(jnp.float32)
        span = slice(tile * LANES, (tile + 1) * LANES)
        att_ref[0:half, span] = jnp.where(low, even, pltpu.roll(odd, HEAD_DIM, 1))
        att_ref[half:tokens, span] = jnp.where(low, pltpu.roll(even, HEAD_DIM, 1), odd)
    att = att_ref[...]
    gained = att * gain_ref[...].astype(jnp.float32)
    target = target_ref[0].astype(jnp.float32)
    weight = 1.0 / (0.1 + jnp.full((1, 1), weight_ref[0], jnp.int32).astype(jnp.float32) / 999.0)
    lane = lax.broadcasted_iota(jnp.int32, (tokens, LANES), 1)

    def over(block):
        return jnp.sum(block, axis=1, keepdims=True)

    table = jnp.where(
        lane == 1,
        over(gained * gained),
        jnp.where(lane == 2, over(gained * target), over(target * target)),
    )
    table = jnp.where(lane == 0, over(att * att), table * weight)
    sums_ref[...] = jnp.broadcast_to(jnp.transpose(table)[None, 0:4, :], sums_ref.shape)


def finish_kernel(heads, att_ref, gain_ref, sums_ref, out_ref, loss_ref):
    tokens, cols = att_ref.shape
    images = sums_ref.shape[0] // heads
    total_cols = cols * heads
    total = None
    for image in range(images):
        sums = jnp.sum(sums_ref[image * heads : (image + 1) * heads], axis=0)
        factor = lax.rsqrt(sums[0:1, :] / total_cols + 1e-06)
        error = factor * factor * sums[1:2, :] - 2.0 * factor * sums[2:3, :] + sums[3:4, :]
        total = error if total is None else total + error
    loss_ref[...] = jnp.broadcast_to(jnp.sum(total, axis=1, keepdims=True)[None], loss_ref.shape)
    own = jnp.sum(sums_ref[pl.ds(lax.axis_index("dp") * heads, heads)], axis=0)
    factor = lax.rsqrt(own[0:1, :] / total_cols + 1e-06)
    column = jnp.transpose(jnp.broadcast_to(factor, (tokens, tokens)))[:, 0:1]
    out_ref[0] = (att_ref[...] * column * gain_ref[...].astype(jnp.float32)).astype(jnp.bfloat16)


def fold_kernel(count, got_ref, sum_ref):
    sum_ref[...] = (jnp.sum(got_ref[...], axis=0) / count)[0:1, 0:1]


def local(
    enc_query,
    enc_key,
    enc_value,
    keep_index,
    keep_count,
    text_key,
    text_value,
    dec_query,
    dec_key,
    mask_value,
    norm_gain,
    target,
    timesteps,
):
    images, seq, heads = (lax.axis_size(name) for name in ("dp", "seq", "head"))
    tokens, cols = enc_query.shape[1:]
    slots = keep_index.shape[1]
    local_heads = cols // HEAD_DIM
    chips = seq // 2
    packed = slots + tokens + slots // 2
    same_core = [[2 * chip + core for chip in range(chips)] for core in range(2)]
    bf16, f32 = jnp.bfloat16, jnp.float32
    gain = norm_gain.reshape(1, cols)

    send = pl.pallas_call(
        pack_kernel,
        out_shape=jax.ShapeDtypeStruct((chips, packed, LANES), bf16),
        in_specs=[pl.BlockSpec(memory_space=pltpu.SMEM)] + [pl.BlockSpec(memory_space=pltpu.HBM)] * 6,
        out_specs=vmem(1)[0],
        scratch_shapes=[pltpu.VMEM((1, slots), jnp.int32)]
        + [pltpu.VMEM((1, tokens, cols), bf16)] * 5
        + [pltpu.SemaphoreType.DMA((6,))],
        compiler_params=params(60),
        name="pack",
    )(keep_count, keep_index, enc_query, enc_key, enc_value, dec_query, dec_key)
    own = lax.all_to_all(send, "seq", 0, 0, axis_index_groups=same_core, tiled=True)
    pair = lax.ppermute(own, "seq", [(source, source ^ 1) for source in range(seq)])
    kept_own = chips * slots
    dec_own = chips * tokens
    begun = pl.pallas_call(
        functools.partial(begin_kernel, slots, tokens),
        out_shape=(
            jax.ShapeDtypeStruct((tokens + kept_own, LANES), bf16),
            jax.ShapeDtypeStruct((tokens + kept_own, LANES), bf16),
            jax.ShapeDtypeStruct((kept_own, LANES), bf16),
            jax.ShapeDtypeStruct((tokens + dec_own, LANES), bf16),
            jax.ShapeDtypeStruct((dec_own, LANES), bf16),
            jax.ShapeDtypeStruct((kept_own, LANES), f32),
            jax.ShapeDtypeStruct((kept_own, LANES), f32),
            jax.ShapeDtypeStruct((8, LANES), f32),
        ),
        in_specs=vmem(4),
        out_specs=tuple(vmem(8)),
        scratch_shapes=[
            pltpu.VMEM((kept_own // 2, tokens + kept_own), f32),
            pltpu.VMEM((kept_own // 2, LANES), f32),
        ]
        * 2,
        compiler_params=params(),
        cost_estimate=pl.CostEstimate(
            flops=4 * kept_own * (tokens + kept_own) * LANES,
            bytes_accessed=8 * MIB,
            transcendentals=kept_own * (tokens + kept_own),
        ),
        name="begin",
    )(own, text_key, text_value, mask_value)
    out = pl.pallas_call(
        functools.partial(attend_kernel, slots, tokens),
        out_shape=jax.ShapeDtypeStruct((chips, tokens // 2, LANES), bf16),
        in_specs=vmem(9),
        out_specs=vmem(1)[0],
        scratch_shapes=[
            pltpu.VMEM((kept_own, LANES), bf16),
            pltpu.VMEM((kept_own, LANES), bf16),
            pltpu.VMEM((kept_own, LANES), bf16),
            pltpu.VMEM((dec_own, LANES), bf16),
            pltpu.VMEM((tokens + 2 * dec_own, LANES), bf16),
        ]
        + [
            pltpu.VMEM((kept_own // 2, tokens + 2 * dec_own), f32),
            pltpu.VMEM((kept_own // 2, LANES), f32),
        ]
        * 2,
        compiler_params=params(),
        name="attend",
    )(pair, *begun)
    got = lax.all_to_all(out, "seq", 0, 0, axis_index_groups=same_core, tiled=True)
    att, sums = pl.pallas_call(
        sums_kernel,
        out_shape=(
            jax.ShapeDtypeStruct((tokens, cols), f32),
            jax.ShapeDtypeStruct((images * heads, 4, tokens), f32),
        ),
        in_specs=vmem(3) + [pl.BlockSpec(memory_space=pltpu.SMEM)],
        out_specs=tuple(vmem(2)),
        compiler_params=params(),
        name="sums",
    )(got, gain, target, timesteps)
    sums = lax.all_to_all(sums, ("dp", "head"), 0, 0, tiled=True)
    decoded, loss = pl.pallas_call(
        functools.partial(finish_kernel, heads),
        out_shape=(
            jax.ShapeDtypeStruct((1, tokens, cols), bf16),
            jax.ShapeDtypeStruct((seq, 1, LANES), f32),
        ),
        in_specs=vmem(3),
        out_specs=tuple(vmem(2)),
        compiler_params=params(),
        name="finish",
    )(att, gain, sums)
    got = lax.all_to_all(loss, "seq", 0, 0, tiled=True)
    loss = pl.pallas_call(
        functools.partial(fold_kernel, float(images * tokens * seq * cols * heads)),
        out_shape=jax.ShapeDtypeStruct((1, 1), f32),
        in_specs=vmem(1),
        out_specs=vmem(1)[0],
        compiler_params=params(),
        name="fold",
    )(got)
    total_loss = loss.reshape(())
    return (decoded, total_loss)


def solution(mesh):
    placed = (
        P("dp", "seq", "head"),
        P("dp", "seq", "head"),
        P("dp", "seq", "head"),
        P("dp", "seq"),
        P("dp", "seq"),
        P("dp", None, "head"),
        P("dp", None, "head"),
        P("dp", "seq", "head"),
        P("dp", "seq", "head"),
        P("head"),
        P("head"),
        P("dp", "seq", "head"),
        P("dp"),
    )
    return jax.shard_map(
        local, mesh=mesh, in_specs=placed, out_specs=(P("dp", "seq", "head"), P()), check_vma=False
    )
```

profile of v0, /device:TPU:1, one launch (start us, length us, event | category | flops | bytes accessed | tf_op | source)
XLA Modules:
  0.0 87.5 jit_solution(10788195610223562525)
XLA Ops:
  1.3 2.3 %pack.1 = bf16[8,272,128]{2,1,0:T(8,128)(2,1)} custom-call(s32[1,1]{1,0:T(1,128)S(6)} %copy.15.count_ref, s32[1,96]{1,0:T(1,128)} %index_hbm.1, bf16[1,128,384]{2,1,0:T(8,128)(2,1)} %eq_hbm.1, bf16[1,128,384]{2,1,0:T(8,128)(2,1)} %ek_hbm.1, bf16[1,128,384]{2,1,0:T(8,128)(2,1)} %ev_hbm.1, bf16[1,128,384]{2,1,0:T(8,128)(2,1)} %dq_hbm.1, ...), custom_call_target="tpu_custom_call" | custom-call | tf_op jit(solution)/shard_map/pack/pallas_call | solution.py:395
  3.6 0.0 copy-start.1
  3.6 0.0 copy-start.2
  3.6 0.0 copy-start.3
  3.6 27.5 %all_to_all.20.own_ref = bf16[8,272,128]{2,1,0:T(8,128)(2,1)S(1)} all-to-all(bf16[8,272,128]{2,1,0:T(8,128)(2,1)} %pack.1), channel_id=1, replica_groups={{0,8,16,24,32,40,48,56},{4,12,20,28,36,44,52,60},{1,9,17,25,33,41,49,57..., dimensions={0} | all-to-all | bytes 1114112 | tf_op jit(solution)/shard_map/all_to_all | solution.py:406
  31.1 4.6 %collective-permute-start = (bf16[8,272,128]{2,1,0:T(8,128)(2,1)S(1)}, bf16[8,272,128]{2,1,0:T(8,128)(2,1)S(1)}, u32[]{:S(2)}, u32[]{:S(2)}) collective-permute-start(bf16[8,272,128]{2,1,0:T(8,128)(2,1)S(1)} %all_to_all.20.own_ref), channel_id=1, source_target_pairs={{0,4},{4,0},{8,12},{12,8},{16,20},{20,16},{24,28},{28,24},{32,36},... | collective-permute-start | bytes 1671176 | tf_op jit(solution)/shard_map/ppermute | solution.py:407
  35.7 0.0 copy-done.1
  35.7 0.0 copy-done.2
  35.7 0.0 copy-done.3
  35.7 1.3 %begin.1 = (bf16[896,128]{1,0:T(8,128)(2,1)S(1)}, bf16[896,128]{1,0:T(8,128)(2,1)S(1)}, bf16[768,128]{1,0:T(8,128)(2,1)S(1)}, bf16[1152,128]{1,0:T(8,128)(2,1)S(...) custom-call(bf16[8,272,128]{2,1,0:T(8,128)(2,1)S(1)} %all_to_all.20., ...), custom_call_target="tpu_custom_call" | custom-call | flops 352321536 | bytes 8388608 | tf_op jit(solution)/shard_map/begin/pallas_call | solution.py:410
  37.0 0.3 collective-permute-done.pair_ref
  37.2 6.1 %attend.1 = bf16[8,64,128]{2,1,0:T(8,128)(2,1)} custom-call(bf16[8,272,128]{2,1,0:T(8,128)(2,1)S(1)} %collective-permute-done.pair_ref, bf16[896,128]{1,0:T(8,128)(2,1)S(1)} %get-tuple-element.14.ek_ref, bf16[896,128]{1,0:T(8,128)(2,1)S(1)} %get-tuple-element.15.ev_ref, bf16[768,128]{1,0:T(8,128)(2,1)S(1)} %get-tuple-element.16.eq_ref, ...), custom_call_target="tpu_custom_call" | custom-call | tf_op jit(solution)/shard_map/attend/pallas_call | solution.py:437
  43.3 0.0 copy-start.4
  43.3 0.0 copy-start
  43.3 3.5 %all-to-all-start.1 = ((bf16[8,64,128]{2,1,0:T(8,128)(2,1)}), bf16[8,64,128]{2,1,0:T(8,128)(2,1)S(1)}, u32[]{:S(2)}, u32[]{:S(2)}) async-start(bf16[8,64,128]{2,1,0:T(8,128)(2,1)} %attend.1), calls=%async_computation.1 | async-start | bytes 262144 | tf_op jit(solution)/shard_map/all_to_all | solution.py:457
  46.8 0.0 copy-done.4
  47.5 7.6 %all-to-all-done.1.got_ref = bf16[8,64,128]{2,1,0:T(8,128)(2,1)S(1)} async-done(((bf16[8,64,128]{2,1,0:T(8,128)(2,1)}), bf16[8,64,128]{2,1,0:T(8,128)(2,1)S(1)}, u32[]{:S(2)}, u32[]{:S(2)}) %all-to-all-start.1) | async-done | bytes 131104 | tf_op jit(solution)/shard_map/all_to_all | solution.py:457
  55.1 0.0 copy-done
  55.1 0.3 sums.1
  55.4 18.3 %all_to_all.21.sums_ref = f32[32,4,128]{2,1,0:T(4,128)S(1)} all-to-all(f32[32,4,128]{2,1,0:T(4,128)S(1)} %get-tuple-element.23), channel_id=1, replica_groups=mesh['dp'=8,'seq'=16,'head'=4] {'dp','head'}, dimensions={0} | all-to-all | bytes 131072 | tf_op jit(solution)/shard_map/all_to_all | solution.py:469
  73.7 0.8 finish.1
  74.5 12.5 %all_to_all.22.got_ref = f32[16,1,128]{2,1,0:T(1,128)S(1)} all-to-all(f32[16,1,128]{2,1,0:T(1,128)S(1)} %get-tuple-element.25), channel_id=1, replica_groups=mesh['dp'=8,'seq'=16,'head'=4] {'seq'}, dimensions={0} | all-to-all | bytes 16384 | tf_op jit(solution)/shard_map/all_to_all | solution.py:481
  87.0 0.5 fold.1
  (1 shorter events, 0.0 us)
Async XLA Ops:
  3.6 32.1 %copy-start.1 = (bf16[1,128,384]{2,1,0:T(8,128)(2,1)S(1)}, bf16[1,128,384]{2,1,0:T(8,128)(2,1)}, u32[]{:S(2)}) copy-start(bf16[1,128,384]{2,1,0:T(8,128)(2,1)} %text_key_ref.1) | copy-start | bytes 294916
  3.6 32.1 %copy-start.2 = (bf16[1,128,384]{2,1,0:T(8,128)(2,1)S(1)}, bf16[1,128,384]{2,1,0:T(8,128)(2,1)}, u32[]{:S(2)}) copy-start(bf16[1,128,384]{2,1,0:T(8,128)(2,1)} %text_value_ref.1) | copy-start | bytes 294916
  3.6 32.1 %copy-start.3 = (bf16[384]{0:T(512)(128)(2,1)S(1)}, bf16[384]{0:T(512)(128)(2,1)}, u32[]{:S(2)}) copy-start(bf16[384]{0:T(512)(128)(2,1)} %mask_ref.1) | copy-start | bytes 2308
  31.1 6.2 %collective-permute-start = (bf16[8,272,128]{2,1,0:T(8,128)(2,1)S(1)}, bf16[8,272,128]{2,1,0:T(8,128)(2,1)S(1)}, u32[]{:S(2)}, u32[]{:S(2)}) collective-permute-start(bf16[8,272,128]{2,1,0:T(8,128)(2,1)S(1)} %all_to_all.20.own_ref), channel_id=1, source_target_pairs={{0,4},{4,0},{8,12},{12,8},{16,20},{20,16},{24,28},{28,24},{32,36},... | collective-permute-start | bytes 1671176 | tf_op jit(solution)/shard_map/ppermute | solution.py:407
  43.3 3.5 %copy-start.4 = (bf16[384]{0:T(512)(128)(2,1)S(1)}, bf16[384]{0:T(512)(128)(2,1)}, u32[]{:S(2)}) copy-start(bf16[384]{0:T(512)(128)(2,1)} %param.23) | copy-start | bytes 2308
  43.3 11.8 %copy-start = (bf16[1,128,384]{2,1,0:T(8,128)(2,1)S(1)}, bf16[1,128,384]{2,1,0:T(8,128)(2,1)}, u32[]{:S(2)}) copy-start(bf16[1,128,384]{2,1,0:T(8,128)(2,1)} %target_ref.1) | copy-start | bytes 294916
  43.3 11.8 %all-to-all-start.1 = ((bf16[8,64,128]{2,1,0:T(8,128)(2,1)}), bf16[8,64,128]{2,1,0:T(8,128)(2,1)S(1)}, u32[]{:S(2)}, u32[]{:S(2)}) async-start(bf16[8,64,128]{2,1,0:T(8,128)(2,1)} %attend.1), calls=%async_computation.1 | async-start | bytes 262144 | tf_op jit(solution)/shard_map/all_to_all | solution.py:457
where the time goes:
time: 88 us; the launch traced here: 87.5 us
  blocking collectives  58.2 us (66%)
  Pallas kernels  11.3 us (13%)
  starting transfers between devices  8.1 us (9%)
  waiting for transfers between devices  7.9 us (9%)
  between operations  2.02 us (2%)
    all_to_all x1, blocking collectives, local(): lax.all_to_all(send, 'seq', 0, 0, axis_index_groups=same_core, tiled=True)  27.5 us
    all_to_all x1, blocking collectives, local(): sums = lax.all_to_all(sums, ('dp', 'head'), 0, 0, tiled=True)  18.3 us
    all_to_all x1, blocking collectives, local(): got = lax.all_to_all(loss, 'seq', 0, 0, tiled=True)  12.5 us
    all_to_all x1, waiting for transfers between devices, local(): lax.all_to_all(out, 'seq', 0, 0, axis_index_groups=same_core, tiled=True)  7.64 us
    pallas_call x1, Pallas kernels, local(): pl.pallas_call(functools.partial(attend_kernel, slots, tokens), out_shape...  6.08 us
    ppermute x1, starting transfers between devices, local(): lax.ppermute(own, 'seq', [(source, source ^ 1) for source in range(seq)])  4.6 us
    all_to_all x1, starting transfers between devices, local(): lax.all_to_all(out, 'seq', 0, 0, axis_index_groups=same_core, tiled=True)  3.5 us
    pallas_call x1, Pallas kernels, local(): pl.pallas_call(pack_kernel, out_shape=jax.ShapeDtypeStruct((chips, packed...  2.29 us
  transfers between devices with their start and end apart: 2, of which 2 were waited for; matrix products, arithmetic and copies ran while one was open for 0% of the time, Pallas kernels for 1%

commit v1 on v0

--- a/solution.py
+++ b/solution.py
@@ -180,6 +180,8 @@
     text_key_ref,
     text_value_ref,
     mask_ref,
+    gain_ref,
+    steps_ref,
     ek_ref,
     ev_ref,
     eq_ref,
@@ -188,6 +190,8 @@
     sums_ref,
     top_ref,
     fill_ref,
+    weight_ref,
+    wide_gain_ref,
     *places
 ):
     chips = own_ref.shape[0]
@@ -209,6 +213,9 @@
     for tile in range(cols // LANES):
         mask_row = jnp.where(head // 2 == tile, whole[:, tile * LANES : (tile + 1) * LANES], mask_row)
     mask_row, _ = low_high(jnp.broadcast_to(mask_row, (8, LANES)))
+    steps = jnp.full((8, LANES), steps_ref[0], jnp.int32).astype(jnp.float32)
+    weight_ref[...] = 1.0 / (0.1 + steps / 999.0)
+    wide_gain_ref[...] = jnp.broadcast_to(gain_ref[...].astype(jnp.float32).reshape(1, cols), (8, cols))
     low = lane_of(tokens) < HEAD_DIM
     fill_ref[...] = jnp.where(lane_of(8) < HEAD_DIM, mask_row, 1.0)
     ek_ref[0:tokens, :] = jnp.where(low, value_low, key_high).astype(jnp.bfloat16)
@@ -329,9 +336,9 @@
         att_ref[0:half, span] = jnp.where(low, even, pltpu.roll(odd, HEAD_DIM, 1))
         att_ref[half:tokens, span] = jnp.where(low, pltpu.roll(even, HEAD_DIM, 1), odd)
     att = att_ref[...]
-    gained = att * gain_ref[...].astype(jnp.float32)
+    gained = att * gain_ref[0:1, :]
     target = target_ref[0].astype(jnp.float32)
-    weight = 1.0 / (0.1 + jnp.full((1, 1), weight_ref[0], jnp.int32).astype(jnp.float32) / 999.0)
+    weight = weight_ref[0:1, :]
     lane = lax.broadcasted_iota(jnp.int32, (tokens, LANES), 1)
 
     def over(block):
@@ -346,25 +353,23 @@
     sums_ref[...] = jnp.broadcast_to(jnp.transpose(table)[None, 0:4, :], sums_ref.shape)
 
 
-def finish_kernel(heads, att_ref, gain_ref, sums_ref, out_ref, loss_ref):
-    tokens, cols = att_ref.shape
-    images = sums_ref.shape[0] // heads
-    total_cols = cols * heads
+def loss_kernel(heads, total_cols, sums_ref, loss_ref):
     total = None
-    for image in range(images):
+    for image in range(sums_ref.shape[0] // heads):
         sums = jnp.sum(sums_ref[image * heads : (image + 1) * heads], axis=0)
         factor = lax.rsqrt(sums[0:1, :] / total_cols + 1e-06)
         error = factor * factor * sums[1:2, :] - 2.0 * factor * sums[2:3, :] + sums[3:4, :]
         total = error if total is None else total + error
     loss_ref[...] = jnp.broadcast_to(jnp.sum(total, axis=1, keepdims=True)[None], loss_ref.shape)
+
+
+def finish_kernel(heads, count, att_ref, gain_ref, sums_ref, got_ref, out_ref, loss_ref):
+    tokens, cols = att_ref.shape
+    loss_ref[...] = (jnp.sum(got_ref[...], axis=0) / count)[0:1, 0:1]
     own = jnp.sum(sums_ref[pl.ds(lax.axis_index("dp") * heads, heads)], axis=0)
-    factor = lax.rsqrt(own[0:1, :] / total_cols + 1e-06)
+    factor = lax.rsqrt(own[0:1, :] / (cols * heads) + 1e-06)
     column = jnp.transpose(jnp.broadcast_to(factor, (tokens, tokens)))[:, 0:1]
-    out_ref[0] = (att_ref[...] * column * gain_ref[...].astype(jnp.float32)).astype(jnp.bfloat16)
-
-
-def fold_kernel(count, got_ref, sum_ref):
-    sum_ref[...] = (jnp.sum(got_ref[...], axis=0) / count)[0:1, 0:1]
+    out_ref[0] = (att_ref[...] * column * gain_ref[0:1, :]).astype(jnp.bfloat16)
 
 
 def local(
@@ -390,7 +395,6 @@
     packed = slots + tokens + slots // 2
     same_core = [[2 * chip + core for chip in range(chips)] for core in range(2)]
     bf16, f32 = jnp.bfloat16, jnp.float32
-    gain = norm_gain.reshape(1, cols)
 
     send = pl.pallas_call(
         pack_kernel,
@@ -407,7 +411,7 @@
     pair = lax.ppermute(own, "seq", [(source, source ^ 1) for source in range(seq)])
     kept_own = chips * slots
     dec_own = chips * tokens
-    begun = pl.pallas_call(
+    *begun, weight, gain = pl.pallas_call(
         functools.partial(begin_kernel, slots, tokens),
         out_shape=(
             jax.ShapeDtypeStruct((tokens + kept_own, LANES), bf16),
@@ -418,9 +422,11 @@
             jax.ShapeDtypeStruct((kept_own, LANES), f32),
             jax.ShapeDtypeStruct((kept_own, LANES), f32),
             jax.ShapeDtypeStruct((8, LANES), f32),
+            jax.ShapeDtypeStruct((8, LANES), f32),
+            jax.ShapeDtypeStruct((8, cols), f32),
         ),
-        in_specs=vmem(4),
-        out_specs=tuple(vmem(8)),
+        in_specs=vmem(5) + [pl.BlockSpec(memory_space=pltpu.SMEM)],
+        out_specs=tuple(vmem(10)),
         scratch_shapes=[
             pltpu.VMEM((kept_own // 2, tokens + kept_own), f32),
             pltpu.VMEM((kept_own // 2, LANES), f32),
@@ -433,7 +439,7 @@
             transcendentals=kept_own * (tokens + kept_own),
         ),
         name="begin",
-    )(own, text_key, text_value, mask_value)
+    )(own, text_key, text_value, mask_value, norm_gain, timesteps)
     out = pl.pallas_call(
         functools.partial(attend_kernel, slots, tokens),
         out_shape=jax.ShapeDtypeStruct((chips, tokens // 2, LANES), bf16),
@@ -461,32 +467,32 @@
             jax.ShapeDtypeStruct((tokens, cols), f32),
             jax.ShapeDtypeStruct((images * heads, 4, tokens), f32),
         ),
-        in_specs=vmem(3) + [pl.BlockSpec(memory_space=pltpu.SMEM)],
+        in_specs=vmem(4),
         out_specs=tuple(vmem(2)),
         compiler_params=params(),
         name="sums",
-    )(got, gain, target, timesteps)
+    )(got, gain, target, weight)
     sums = lax.all_to_all(sums, ("dp", "head"), 0, 0, tiled=True)
+    loss = pl.pallas_call(
+        functools.partial(loss_kernel, heads, cols * heads),
+        out_shape=jax.ShapeDtypeStruct((seq, 1, LANES), f32),
+        in_specs=vmem(1),
+        out_specs=vmem(1)[0],
+        compiler_params=params(),
+        name="loss",
+    )(sums)
+    got = lax.all_to_all(loss, "seq", 0, 0, tiled=True)
     decoded, loss = pl.pallas_call(
-        functools.partial(finish_kernel, heads),
+        functools.partial(finish_kernel, heads, float(images * tokens * seq * cols * heads)),
         out_shape=(
             jax.ShapeDtypeStruct((1, tokens, cols), bf16),
-            jax.ShapeDtypeStruct((seq, 1, LANES), f32),
+            jax.ShapeDtypeStruct((1, 1), f32),
         ),
-        in_specs=vmem(3),
+        in_specs=vmem(4),
         out_specs=tuple(vmem(2)),
         compiler_params=params(),
         name="finish",
-    )(att, gain, sums)
-    got = lax.all_to_all(loss, "seq", 0, 0, tiled=True)
-    loss = pl.pallas_call(
-        functools.partial(fold_kernel, float(images * tokens * seq * cols * heads)),
-        out_shape=jax.ShapeDtypeStruct((1, 1), f32),
-        in_specs=vmem(1),
-        out_specs=vmem(1)[0],
-        compiler_params=params(),
-        name="fold",
-    )(got)
+    )(att, gain, sums, got)
     total_loss = loss.reshape(())
     return (decoded, total_loss)
 

time: 88 us -> 86.6 us (0.984)
  blocking collectives: 58.2 us -> 69.1 us
  waiting for transfers between devices: 7.9 us -> 0.01 us
  starting transfers between devices: 8.1 us -> 4.73 us
  Pallas kernels: 11.3 us -> 10.2 us
    all_to_all x0 -> x1, blocking collectives: none -> 12 us  [local(): lax.all_to_all(out, 'seq', 0, 0, axis_index_groups=same_core, tiled=True)]
    all_to_all x1 -> x0, waiting for transfers between devices: 7.64 us -> none  [local(): lax.all_to_all(out, 'seq', 0, 0, axis_index_groups=same_core, tiled=True)]
    all_to_all x1 -> x0, starting transfers between devices: 3.5 us -> none  [local(): lax.all_to_all(out, 'seq', 0, 0, axis_index_groups=same_core, tiled=True)]
    all_to_all x1, blocking collectives: 12.5 us -> 11.3 us  [local(): got = lax.all_to_all(loss, 'seq', 0, 0, tiled=True)]
  transfers between devices with their start and end apart: 2 -> 1, of which waited for: 2 -> 0; matrix products, arithmetic and copies ran while one was open for 0% -> 0% of each run, Pallas kernels for 1% -> 1%
where the time goes in v1:
time: 86.6 us; the launch traced here: 86.2 us
  blocking collectives  69.1 us (80%)
  Pallas kernels  10.2 us (12%)
  starting transfers between devices  4.73 us (5%)
  between operations  2.02 us (2%)
    all_to_all x1, blocking collectives, local(): lax.all_to_all(send, 'seq', 0, 0, axis_index_groups=same_core, tiled=True)  27.5 us
    all_to_all x1, blocking collectives, local(): sums = lax.all_to_all(sums, ('dp', 'head'), 0, 0, tiled=True)  18.4 us
    all_to_all x1, blocking collectives, local(): lax.all_to_all(out, 'seq', 0, 0, axis_index_groups=same_core, tiled=True)  12 us
    all_to_all x1, blocking collectives, local(): got = lax.all_to_all(loss, 'seq', 0, 0, tiled=True)  11.3 us
    pallas_call x1, Pallas kernels, local(): pl.pallas_call(functools.partial(attend_kernel, slots, tokens), out_shape...  5.46 us
    ppermute x1, starting transfers between devices, local(): lax.ppermute(own, 'seq', [(source, source ^ 1) for source in range(seq)])  4.73 us
    pallas_call x1, Pallas kernels, local(): pl.pallas_call(pack_kernel, out_shape=jax.ShapeDtypeStruct((chips, packed...  2.29 us
  transfers between devices with their start and end apart: 1, of which 0 were waited for; matrix products, arithmetic and copies ran while one was open for 0% of the time, Pallas kernels for 1%

profile of v1, /device:TPU:1, one launch (start us, length us, event | category | flops | bytes accessed | tf_op | source)
XLA Modules:
  0.0 86.2 jit_solution(4719218599177453421)
XLA Ops:
  1.3 2.3 %pack.1 = bf16[8,272,128]{2,1,0:T(8,128)(2,1)} custom-call(s32[1,1]{1,0:T(1,128)S(6)} %copy.15.count_ref, s32[1,96]{1,0:T(1,128)} %index_hbm.1, bf16[1,128,384]{2,1,0:T(8,128)(2,1)} %eq_hbm.1, bf16[1,128,384]{2,1,0:T(8,128)(2,1)} %ek_hbm.1, bf16[1,128,384]{2,1,0:T(8,128)(2,1)} %ev_hbm.1, bf16[1,128,384]{2,1,0:T(8,128)(2,1)} %dq_hbm.1, ...), custom_call_target="tpu_custom_call" | custom-call | tf_op jit(solution)/shard_map/pack/pallas_call | solution.py:399
  3.6 0.0 copy-start.1
  3.6 0.0 copy-start.2
  3.6 0.0 copy-start.4
  3.6 27.5 %all_to_all.20.own_ref = bf16[8,272,128]{2,1,0:T(8,128)(2,1)S(1)} all-to-all(bf16[8,272,128]{2,1,0:T(8,128)(2,1)} %pack.1), channel_id=1, replica_groups={{0,8,16,24,32,40,48,56},{4,12,20,28,36,44,52,60},{1,9,17,25,33,41,49,57..., dimensions={0} | all-to-all | bytes 1114112 | tf_op jit(solution)/shard_map/all_to_all | solution.py:410
  31.1 0.0 copy-start.3
  31.1 4.7 %collective-permute-start = (bf16[8,272,128]{2,1,0:T(8,128)(2,1)S(1)}, bf16[8,272,128]{2,1,0:T(8,128)(2,1)S(1)}, u32[]{:S(2)}, u32[]{:S(2)}) collective-permute-start(bf16[8,272,128]{2,1,0:T(8,128)(2,1)S(1)} %all_to_all.20.own_ref), channel_id=1, source_target_pairs={{0,4},{4,0},{8,12},{12,8},{16,20},{20,16},{24,28},{28,24},{32,36},... | collective-permute-start | bytes 1671176 | tf_op jit(solution)/shard_map/ppermute | solution.py:411
  36.4 0.0 copy-done.1
  36.5 0.0 copy-done.2
  36.5 0.0 copy-done.4
  36.5 0.0 copy-done.3
  36.5 1.3 %begin.1 = (bf16[896,128]{1,0:T(8,128)(2,1)S(1)}, bf16[896,128]{1,0:T(8,128)(2,1)S(1)}, bf16[768,128]{1,0:T(8,128)(2,1)S(1)}, bf16[1152,128]{1,0:T(8,128)(2,1)S(...) custom-call(bf16[8,272,128]{2,1,0:T(8,128)(2,1)S(1)} %all_to_all.20., ...), custom_call_target="tpu_custom_call" | custom-call | flops 352321536 | bytes 8388608 | tf_op jit(solution)/shard_map/begin/pallas_call | solution.py:414
  37.8 0.0 collective-permute-done.pair_ref
  37.8 5.5 %attend.1 = bf16[8,64,128]{2,1,0:T(8,128)(2,1)S(1)} custom-call(bf16[8,272,128]{2,1,0:T(8,128)(2,1)S(1)} %collective-permute-done.pair_ref, bf16[896,128]{1,0:T(8,128)(2,1)S(1)} %get-tuple-element.16.ek_ref, bf16[896,128]{1,0:T(8,128)(2,1)S(1)} %get-tuple-element.17.ev_ref, bf16[768,128]{1,0:T(8,128)(2,1)S(1)} %get-tuple-element.18.eq_ref, ...), custom_call_target="tpu_custom_call" | custom-call | tf_op jit(solution)/shard_map/attend/pallas_call | solution.py:443
  43.2 0.0 copy-start
  43.2 12.0 %all_to_all.21.got_ref = bf16[8,64,128]{2,1,0:T(8,128)(2,1)S(1)} all-to-all(bf16[8,64,128]{2,1,0:T(8,128)(2,1)S(1)} %attend.1), channel_id=1, replica_groups={{0,8,16,24,32,40,48,56},{4,12,20,28,36,44,52,60},{1,9,17,25,33,41,49,57..., dimensions={0} | all-to-all | bytes 262144 | tf_op jit(solution)/shard_map/all_to_all | solution.py:463
  55.2 0.0 copy-done
  55.2 0.3 sums.1
  55.5 18.4 %all_to_all.22.sums_ref = f32[32,4,128]{2,1,0:T(4,128)S(1)} all-to-all(f32[32,4,128]{2,1,0:T(4,128)S(1)} %get-tuple-element.27), channel_id=1, replica_groups=mesh['dp'=8,'seq'=16,'head'=4] {'dp','head'}, dimensions={0} | all-to-all | bytes 131072 | tf_op jit(solution)/shard_map/all_to_all | solution.py:475
  73.9 0.1 loss.1
  74.0 11.3 %all_to_all.23.got_ref = f32[16,1,128]{2,1,0:T(1,128)S(1)} all-to-all(f32[16,1,128]{2,1,0:T(1,128)S(1)} %loss.1), channel_id=1, replica_groups=mesh['dp'=8,'seq'=16,'head'=4] {'seq'}, dimensions={0} | all-to-all | bytes 16384 | tf_op jit(solution)/shard_map/all_to_all | solution.py:484
  85.3 0.8 finish.1
Async XLA Ops:
  3.6 32.9 %copy-start.1 = (bf16[1,128,384]{2,1,0:T(8,128)(2,1)S(1)}, bf16[1,128,384]{2,1,0:T(8,128)(2,1)}, u32[]{:S(2)}) copy-start(bf16[1,128,384]{2,1,0:T(8,128)(2,1)} %text_key_ref.1) | copy-start | bytes 294916
  3.6 32.9 %copy-start.2 = (bf16[1,128,384]{2,1,0:T(8,128)(2,1)S(1)}, bf16[1,128,384]{2,1,0:T(8,128)(2,1)}, u32[]{:S(2)}) copy-start(bf16[1,128,384]{2,1,0:T(8,128)(2,1)} %text_value_ref.1) | copy-start | bytes 294916
  3.6 32.9 %copy-start.4 = (bf16[384]{0:T(512)(128)(2,1)S(1)}, bf16[384]{0:T(512)(128)(2,1)}, u32[]{:S(2)}) copy-start(bf16[384]{0:T(512)(128)(2,1)} %gain_ref.1) | copy-start | bytes 2308
  31.1 5.4 %copy-start.3 = (bf16[384]{0:T(512)(128)(2,1)S(1)}, bf16[384]{0:T(512)(128)(2,1)}, u32[]{:S(2)}) copy-start(bf16[384]{0:T(512)(128)(2,1)} %mask_ref.1) | copy-start | bytes 2308
  31.1 6.7 %collective-permute-start = (bf16[8,272,128]{2,1,0:T(8,128)(2,1)S(1)}, bf16[8,272,128]{2,1,0:T(8,128)(2,1)S(1)}, u32[]{:S(2)}, u32[]{:S(2)}) collective-permute-start(bf16[8,272,128]{2,1,0:T(8,128)(2,1)S(1)} %all_to_all.20.own_ref), channel_id=1, source_target_pairs={{0,4},{4,0},{8,12},{12,8},{16,20},{20,16},{24,28},{28,24},{32,36},... | collective-permute-start | bytes 1671176 | tf_op jit(solution)/shard_map/ppermute | solution.py:411
  43.2 12.0 %copy-start = (bf16[1,128,384]{2,1,0:T(8,128)(2,1)S(1)}, bf16[1,128,384]{2,1,0:T(8,128)(2,1)}, u32[]{:S(2)}) copy-start(bf16[1,128,384]{2,1,0:T(8,128)(2,1)} %target_ref.1) | copy-start | bytes 294916

commit v2 on v1

--- a/solution.py
+++ b/solution.py
@@ -29,7 +29,7 @@
 
 
 def pack_kernel(
-    count_ref, index_hbm, eq_hbm, ek_hbm, ev_hbm, dq_hbm, dk_hbm, send_ref, *scratch
+    index_hbm, eq_hbm, ek_hbm, ev_hbm, dq_hbm, dk_hbm, send_ref, *scratch
 ):
     *held, sems = scratch
     given = (index_hbm, eq_hbm, ek_hbm, ev_hbm, dq_hbm, dk_hbm)
@@ -45,12 +45,11 @@
     slots = index_ref.shape[1]
     heads = cols // HEAD_DIM
     spare = tokens - slots
-    total = count_ref[0, 0]
     index = jnp.broadcast_to(index_ref[...].astype(jnp.float32), (tokens, slots))
     index = jnp.transpose(index)
     token = lax.broadcasted_iota(jnp.int32, (slots, tokens), 1).astype(jnp.float32)
     slot = lax.broadcasted_iota(jnp.int32, (slots, tokens), 0)
-    live = slot < total
+    live = (slot == 0) | (index > 0.5)
     match_live = jnp.where(live & (token == index), 1.0, 0.0)
     match_fill = jnp.where(token == jnp.where(live, index, index[0:1, :]), 1.0, 0.0)
     kept = jnp.sum(match_live, axis=0, keepdims=True)
@@ -60,7 +59,7 @@
     before = jnp.where(row < col, 1.0, 0.0).astype(jnp.bfloat16)
     left = jnp.broadcast_to(1.0 - kept, (16, tokens)).astype(jnp.bfloat16)
     rank = one_hot_dot(left, before)[0:1, :]
-    place = jnp.where(kept > 0.5, kept_slot, total.astype(jnp.float32) + rank)
+    place = jnp.where(kept > 0.5, kept_slot, jnp.sum(kept, axis=1, keepdims=True) + rank)
     order = jnp.where(row.astype(jnp.float32) == place, 1.0, 0.0).astype(jnp.bfloat16)
 
     for copy in copies[1:]:
@@ -69,8 +68,8 @@
     match_live = match_live.astype(jnp.bfloat16)
     match_fill = match_fill.astype(jnp.bfloat16)
     query = one_hot_dot(match_live, eq_ref[0]) * scale
-    slot_wide = lax.broadcasted_iota(jnp.int32, (slots, cols), 0)
-    query = jnp.where(slot_wide < total, query, DEAD)
+    dead = jnp.where(live, 0.0, DEAD)
+    query = query + jnp.concatenate([dead] * (cols // tokens), axis=1)
     key = one_hot_dot(match_fill, ek_ref[0])
     value = one_hot_dot(match_live, ev_ref[0])
     dec_key = one_hot_dot(order, dk_ref[0])
@@ -399,14 +398,14 @@
     send = pl.pallas_call(
         pack_kernel,
         out_shape=jax.ShapeDtypeStruct((chips, packed, LANES), bf16),
-        in_specs=[pl.BlockSpec(memory_space=pltpu.SMEM)] + [pl.BlockSpec(memory_space=pltpu.HBM)] * 6,
+        in_specs=[pl.BlockSpec(memory_space=pltpu.HBM)] * 6,
         out_specs=vmem(1)[0],
         scratch_shapes=[pltpu.VMEM((1, slots), jnp.int32)]
         + [pltpu.VMEM((1, tokens, cols), bf16)] * 5
         + [pltpu.SemaphoreType.DMA((6,))],
         compiler_params=params(60),
         name="pack",
-    )(keep_count, keep_index, enc_query, enc_key, enc_value, dec_query, dec_key)
+    )(keep_index, enc_query, enc_key, enc_value, dec_query, dec_key)
     own = lax.all_to_all(send, "seq", 0, 0, axis_index_groups=same_core, tiled=True)
     pair = lax.ppermute(own, "seq", [(source, source ^ 1) for source in range(seq)])
     kept_own = chips * slots

time: 86.6 us -> 85.9 us (level)
  no operation moved by 1% of the time
where the time goes in v2:
time: 85.9 us; the launch traced here: 85.5 us
  blocking collectives  69.1 us (80%)
  Pallas kernels  10.2 us (12%)
  starting transfers between devices  4.73 us (6%)
  between operations  1.37 us (2%)
    all_to_all x1, blocking collectives, local(): lax.all_to_all(send, 'seq', 0, 0, axis_index_groups=same_core, tiled=True)  27.5 us
    all_to_all x1, blocking collectives, local(): sums = lax.all_to_all(sums, ('dp', 'head'), 0, 0, tiled=True)  18.4 us
    all_to_all x1, blocking collectives, local(): lax.all_to_all(out, 'seq', 0, 0, axis_index_groups=same_core, tiled=True)  12 us
    all_to_all x1, blocking collectives, local(): got = lax.all_to_all(loss, 'seq', 0, 0, tiled=True)  11.3 us
    pallas_call x1, Pallas kernels, local(): pl.pallas_call(functools.partial(attend_kernel, slots, tokens), out_shape...  5.45 us
    ppermute x1, starting transfers between devices, local(): lax.ppermute(own, 'seq', [(source, source ^ 1) for source in range(seq)])  4.73 us
    pallas_call x1, Pallas kernels, local(): pl.pallas_call(pack_kernel, out_shape=jax.ShapeDtypeStruct((chips, packed...  2.29 us
  transfers between devices with their start and end apart: 1, of which 0 were waited for; matrix products, arithmetic and copies ran while one was open for 0% of the time, Pallas kernels for 1%

profile of v2, /device:TPU:1, one launch (start us, length us, event | category | flops | bytes accessed | tf_op | source)
XLA Modules:
  0.0 85.5 jit_solution(14553075957286387969)
XLA Ops:
  0.6 2.3 %pack.1 = bf16[8,272,128]{2,1,0:T(8,128)(2,1)} custom-call(s32[1,96]{1,0:T(1,128)} %index_hbm.1, bf16[1,128,384]{2,1,0:T(8,128)(2,1)} %eq_hbm.1, bf16[1,128,384]{2,1,0:T(8,128)(2,1)} %ek_hbm.1, bf16[1,128,384]{2,1,0:T(8,128)(2,1)} %ev_hbm.1, bf16[1,128,384]{2,1,0:T(8,128)(2,1)} %dq_hbm.1, bf16[1,128,384]{2,1,0:T(8,128)(2,1)} %dk_hbm.1), custom_call_target="tpu_custom_call" | custom-call | tf_op jit(solution)/shard_map/pack/pallas_call | solution.py:398
  2.9 0.0 copy-start.1
  2.9 0.0 copy-start.2
  2.9 0.0 copy-start.4
  3.0 27.5 %all_to_all.20.own_ref = bf16[8,272,128]{2,1,0:T(8,128)(2,1)S(1)} all-to-all(bf16[8,272,128]{2,1,0:T(8,128)(2,1)} %pack.1), channel_id=1, replica_groups={{0,8,16,24,32,40,48,56},{4,12,20,28,36,44,52,60},{1,9,17,25,33,41,49,57..., dimensions={0} | all-to-all | bytes 1114112 | tf_op jit(solution)/shard_map/all_to_all | solution.py:409
  30.4 0.0 copy-start.3
  30.4 4.7 %collective-permute-start = (bf16[8,272,128]{2,1,0:T(8,128)(2,1)S(1)}, bf16[8,272,128]{2,1,0:T(8,128)(2,1)S(1)}, u32[]{:S(2)}, u32[]{:S(2)}) collective-permute-start(bf16[8,272,128]{2,1,0:T(8,128)(2,1)S(1)} %all_to_all.20.own_ref), channel_id=1, source_target_pairs={{0,4},{4,0},{8,12},{12,8},{16,20},{20,16},{24,28},{28,24},{32,36},... | collective-permute-start | bytes 1671176 | tf_op jit(solution)/shard_map/ppermute | solution.py:410
  35.8 0.0 copy-done.1
  35.8 0.0 copy-done.2
  35.8 0.0 copy-done.4
  35.8 0.0 copy-done.3
  35.8 1.3 %begin.1 = (bf16[896,128]{1,0:T(8,128)(2,1)S(1)}, bf16[896,128]{1,0:T(8,128)(2,1)S(1)}, bf16[768,128]{1,0:T(8,128)(2,1)S(1)}, bf16[1152,128]{1,0:T(8,128)(2,1)S(...) custom-call(bf16[8,272,128]{2,1,0:T(8,128)(2,1)S(1)} %all_to_all.20., ...), custom_call_target="tpu_custom_call" | custom-call | flops 352321536 | bytes 8388608 | tf_op jit(solution)/shard_map/begin/pallas_call | solution.py:413
  37.1 0.0 collective-permute-done.pair_ref
  37.1 5.5 %attend.1 = bf16[8,64,128]{2,1,0:T(8,128)(2,1)S(1)} custom-call(bf16[8,272,128]{2,1,0:T(8,128)(2,1)S(1)} %collective-permute-done.pair_ref, bf16[896,128]{1,0:T(8,128)(2,1)S(1)} %get-tuple-element.16.ek_ref, bf16[896,128]{1,0:T(8,128)(2,1)S(1)} %get-tuple-element.17.ev_ref, bf16[768,128]{1,0:T(8,128)(2,1)S(1)} %get-tuple-element.18.eq_ref, ...), custom_call_target="tpu_custom_call" | custom-call | tf_op jit(solution)/shard_map/attend/pallas_call | solution.py:442
  42.6 0.0 copy-start
  42.6 12.0 %all_to_all.21.got_ref = bf16[8,64,128]{2,1,0:T(8,128)(2,1)S(1)} all-to-all(bf16[8,64,128]{2,1,0:T(8,128)(2,1)S(1)} %attend.1), channel_id=1, replica_groups={{0,8,16,24,32,40,48,56},{4,12,20,28,36,44,52,60},{1,9,17,25,33,41,49,57..., dimensions={0} | all-to-all | bytes 262144 | tf_op jit(solution)/shard_map/all_to_all | solution.py:462
  54.6 0.0 copy-done
  54.6 0.3 sums.1
  54.9 18.4 %all_to_all.22.sums_ref = f32[32,4,128]{2,1,0:T(4,128)S(1)} all-to-all(f32[32,4,128]{2,1,0:T(4,128)S(1)} %get-tuple-element.27), channel_id=1, replica_groups=mesh['dp'=8,'seq'=16,'head'=4] {'dp','head'}, dimensions={0} | all-to-all | bytes 131072 | tf_op jit(solution)/shard_map/all_to_all | solution.py:474
  73.2 0.1 loss.1
  73.3 11.3 %all_to_all.23.got_ref = f32[16,1,128]{2,1,0:T(1,128)S(1)} all-to-all(f32[16,1,128]{2,1,0:T(1,128)S(1)} %loss.1), channel_id=1, replica_groups=mesh['dp'=8,'seq'=16,'head'=4] {'seq'}, dimensions={0} | all-to-all | bytes 16384 | tf_op jit(solution)/shard_map/all_to_all | solution.py:483
  84.7 0.8 finish.1
Async XLA Ops:
  2.9 32.9 %copy-start.1 = (bf16[1,128,384]{2,1,0:T(8,128)(2,1)S(1)}, bf16[1,128,384]{2,1,0:T(8,128)(2,1)}, u32[]{:S(2)}) copy-start(bf16[1,128,384]{2,1,0:T(8,128)(2,1)} %text_key_ref.1) | copy-start | bytes 294916
  2.9 32.9 %copy-start.2 = (bf16[1,128,384]{2,1,0:T(8,128)(2,1)S(1)}, bf16[1,128,384]{2,1,0:T(8,128)(2,1)}, u32[]{:S(2)}) copy-start(bf16[1,128,384]{2,1,0:T(8,128)(2,1)} %text_value_ref.1) | copy-start | bytes 294916
  2.9 32.9 %copy-start.4 = (bf16[384]{0:T(512)(128)(2,1)S(1)}, bf16[384]{0:T(512)(128)(2,1)}, u32[]{:S(2)}) copy-start(bf16[384]{0:T(512)(128)(2,1)} %gain_ref.1) | copy-start | bytes 2308
  30.4 5.4 %copy-start.3 = (bf16[384]{0:T(512)(128)(2,1)S(1)}, bf16[384]{0:T(512)(128)(2,1)}, u32[]{:S(2)}) copy-start(bf16[384]{0:T(512)(128)(2,1)} %mask_ref.1) | copy-start | bytes 2308
  30.4 6.7 %collective-permute-start = (bf16[8,272,128]{2,1,0:T(8,128)(2,1)S(1)}, bf16[8,272,128]{2,1,0:T(8,128)(2,1)S(1)}, u32[]{:S(2)}, u32[]{:S(2)}) collective-permute-start(bf16[8,272,128]{2,1,0:T(8,128)(2,1)S(1)} %all_to_all.20.own_ref), channel_id=1, source_target_pairs={{0,4},{4,0},{8,12},{12,8},{16,20},{20,16},{24,28},{28,24},{32,36},... | collective-permute-start | bytes 1671176 | tf_op jit(solution)/shard_map/ppermute | solution.py:410
  42.6 12.0 %copy-start = (bf16[1,128,384]{2,1,0:T(8,128)(2,1)S(1)}, bf16[1,128,384]{2,1,0:T(8,128)(2,1)}, u32[]{:S(2)}) copy-start(bf16[1,128,384]{2,1,0:T(8,128)(2,1)} %target_ref.1) | copy-start | bytes 294916

commit v3 on v2

--- a/solution.py
+++ b/solution.py
@@ -354,8 +354,8 @@
 
 def loss_kernel(heads, total_cols, sums_ref, loss_ref):
     total = None
-    for image in range(sums_ref.shape[0] // heads):
-        sums = jnp.sum(sums_ref[image * heads : (image + 1) * heads], axis=0)
+    for chip in range(sums_ref.shape[0] // heads):
+        sums = jnp.sum(sums_ref[chip * heads : (chip + 1) * heads], axis=0)
         factor = lax.rsqrt(sums[0:1, :] / total_cols + 1e-06)
         error = factor * factor * sums[1:2, :] - 2.0 * factor * sums[2:3, :] + sums[3:4, :]
         total = error if total is None else total + error
@@ -365,7 +365,7 @@
 def finish_kernel(heads, count, att_ref, gain_ref, sums_ref, got_ref, out_ref, loss_ref):
     tokens, cols = att_ref.shape
     loss_ref[...] = (jnp.sum(got_ref[...], axis=0) / count)[0:1, 0:1]
-    own = jnp.sum(sums_ref[pl.ds(lax.axis_index("dp") * heads, heads)], axis=0)
+    own = jnp.sum(sums_ref[pl.ds(lax.axis_index("seq") // 2 * heads, heads)], axis=0)
     factor = lax.rsqrt(own[0:1, :] / (cols * heads) + 1e-06)
     column = jnp.transpose(jnp.broadcast_to(factor, (tokens, tokens)))[:, 0:1]
     out_ref[0] = (att_ref[...] * column * gain_ref[0:1, :]).astype(jnp.bfloat16)
@@ -464,23 +464,29 @@
         sums_kernel,
         out_shape=(
             jax.ShapeDtypeStruct((tokens, cols), f32),
-            jax.ShapeDtypeStruct((images * heads, 4, tokens), f32),
+            jax.ShapeDtypeStruct((chips * heads, 4, tokens), f32),
         ),
         in_specs=vmem(4),
         out_specs=tuple(vmem(2)),
         compiler_params=params(),
         name="sums",
     )(got, gain, target, weight)
-    sums = lax.all_to_all(sums, ("dp", "head"), 0, 0, tiled=True)
+    planes = [
+        [(2 * chip + core) * heads + head for chip in range(chips) for head in range(heads)] for core in range(2)
+    ]
+    sums = lax.all_to_all(sums, ("seq", "head"), 0, 0, axis_index_groups=planes, tiled=True)
     loss = pl.pallas_call(
         functools.partial(loss_kernel, heads, cols * heads),
-        out_shape=jax.ShapeDtypeStruct((seq, 1, LANES), f32),
+        out_shape=jax.ShapeDtypeStruct((2 * images, 1, LANES), f32),
         in_specs=vmem(1),
         out_specs=vmem(1)[0],
         compiler_params=params(),
         name="loss",
     )(sums)
-    got = lax.all_to_all(loss, "seq", 0, 0, tiled=True)
+    columns = [
+        [image * seq + 2 * chip + core for image in range(images) for core in range(2)] for chip in range(chips)
+    ]
+    got = lax.all_to_all(loss, ("dp", "seq"), 0, 0, axis_index_groups=columns, tiled=True)
     decoded, loss = pl.pallas_call(
         functools.partial(finish_kernel, heads, float(images * tokens * seq * cols * heads)),
         out_shape=(

time: 85.9 us -> 85.1 us (level)
  no operation moved by 1% of the time
where the time goes in v3:
time: 85.1 us; the launch traced here: 84.7 us
  blocking collectives  68.4 us (80%)
  Pallas kernels  10.2 us (12%)
  starting transfers between devices  4.73 us (6%)
  between operations  1.37 us (2%)
    all_to_all x1, blocking collectives, local(): lax.all_to_all(send, 'seq', 0, 0, axis_index_groups=same_core, tiled=True)  27.5 us
    all_to_all x1, blocking collectives, local(): lax.all_to_all(loss, ('dp', 'seq'), 0, 0, axis_index_groups=columns, tile...  15.8 us
    all_to_all x1, blocking collectives, local(): lax.all_to_all(sums, ('seq', 'head'), 0, 0, axis_index_groups=planes, til...  13.1 us
    all_to_all x1, blocking collectives, local(): lax.all_to_all(out, 'seq', 0, 0, axis_index_groups=same_core, tiled=True)  12 us
    pallas_call x1, Pallas kernels, local(): pl.pallas_call(functools.partial(attend_kernel, slots, tokens), out_shape...  5.45 us
    ppermute x1, starting transfers between devices, local(): lax.ppermute(own, 'seq', [(source, source ^ 1) for source in range(seq)])  4.73 us
    pallas_call x1, Pallas kernels, local(): pl.pallas_call(pack_kernel, out_shape=jax.ShapeDtypeStruct((chips, packed...  2.29 us
  transfers between devices with their start and end apart: 1, of which 0 were waited for; matrix products, arithmetic and copies ran while one was open for 0% of the time, Pallas kernels for 1%

profile of v3, /device:TPU:1, one launch (start us, length us, event | category | flops | bytes accessed | tf_op | source)
XLA Modules:
  0.0 84.7 jit_solution(6776158743018206078)
XLA Ops:
  0.6 2.3 %pack.1 = bf16[8,272,128]{2,1,0:T(8,128)(2,1)} custom-call(s32[1,96]{1,0:T(1,128)} %index_hbm.1, bf16[1,128,384]{2,1,0:T(8,128)(2,1)} %eq_hbm.1, bf16[1,128,384]{2,1,0:T(8,128)(2,1)} %ek_hbm.1, bf16[1,128,384]{2,1,0:T(8,128)(2,1)} %ev_hbm.1, bf16[1,128,384]{2,1,0:T(8,128)(2,1)} %dq_hbm.1, bf16[1,128,384]{2,1,0:T(8,128)(2,1)} %dk_hbm.1), custom_call_target="tpu_custom_call" | custom-call | tf_op jit(solution)/shard_map/pack/pallas_call | solution.py:398
  2.9 0.0 copy-start.1
  2.9 0.0 copy-start.2
  2.9 0.0 copy-start.4
  3.0 27.5 %all_to_all.20.own_ref = bf16[8,272,128]{2,1,0:T(8,128)(2,1)S(1)} all-to-all(bf16[8,272,128]{2,1,0:T(8,128)(2,1)} %pack.1), channel_id=1, replica_groups={{0,8,16,24,32,40,48,56},{4,12,20,28,36,44,52,60},{1,9,17,25,33,41,49,57..., dimensions={0} | all-to-all | bytes 1114112 | tf_op jit(solution)/shard_map/all_to_all | solution.py:409
  30.4 0.0 copy-start.3
  30.4 4.7 %collective-permute-start = (bf16[8,272,128]{2,1,0:T(8,128)(2,1)S(1)}, bf16[8,272,128]{2,1,0:T(8,128)(2,1)S(1)}, u32[]{:S(2)}, u32[]{:S(2)}) collective-permute-start(bf16[8,272,128]{2,1,0:T(8,128)(2,1)S(1)} %all_to_all.20.own_ref), channel_id=1, source_target_pairs={{0,4},{4,0},{8,12},{12,8},{16,20},{20,16},{24,28},{28,24},{32,36},... | collective-permute-start | bytes 1671176 | tf_op jit(solution)/shard_map/ppermute | solution.py:410
  35.8 0.0 copy-done.1
  35.8 0.0 copy-done.2
  35.8 0.0 copy-done.4
  35.8 0.0 copy-done.3
  35.8 1.3 %begin.1 = (bf16[896,128]{1,0:T(8,128)(2,1)S(1)}, bf16[896,128]{1,0:T(8,128)(2,1)S(1)}, bf16[768,128]{1,0:T(8,128)(2,1)S(1)}, bf16[1152,128]{1,0:T(8,128)(2,1)S(...) custom-call(bf16[8,272,128]{2,1,0:T(8,128)(2,1)S(1)} %all_to_all.20., ...), custom_call_target="tpu_custom_call" | custom-call | flops 352321536 | bytes 8388608 | tf_op jit(solution)/shard_map/begin/pallas_call | solution.py:413
  37.1 0.0 collective-permute-done.pair_ref
  37.1 5.5 %attend.1 = bf16[8,64,128]{2,1,0:T(8,128)(2,1)S(1)} custom-call(bf16[8,272,128]{2,1,0:T(8,128)(2,1)S(1)} %collective-permute-done.pair_ref, bf16[896,128]{1,0:T(8,128)(2,1)S(1)} %get-tuple-element.16.ek_ref, bf16[896,128]{1,0:T(8,128)(2,1)S(1)} %get-tuple-element.17.ev_ref, bf16[768,128]{1,0:T(8,128)(2,1)S(1)} %get-tuple-element.18.eq_ref, ...), custom_call_target="tpu_custom_call" | custom-call | tf_op jit(solution)/shard_map/attend/pallas_call | solution.py:442
  42.6 0.0 copy-start
  42.6 12.0 %all_to_all.21.got_ref = bf16[8,64,128]{2,1,0:T(8,128)(2,1)S(1)} all-to-all(bf16[8,64,128]{2,1,0:T(8,128)(2,1)S(1)} %attend.1), channel_id=1, replica_groups={{0,8,16,24,32,40,48,56},{4,12,20,28,36,44,52,60},{1,9,17,25,33,41,49,57..., dimensions={0} | all-to-all | bytes 262144 | tf_op jit(solution)/shard_map/all_to_all | solution.py:462
  54.6 0.0 copy-done
  54.6 0.3 sums.1
  54.9 13.1 %all_to_all.22.sums_ref = f32[32,4,128]{2,1,0:T(4,128)S(1)} all-to-all(f32[32,4,128]{2,1,0:T(4,128)S(1)} %get-tuple-element.27), channel_id=1, replica_groups={{0,1,2,3,8,9,10,11,16,17,18,19,24,25,26,27,32,33,34,35,40,41,42,43,48,4..., dimensions={0} | all-to-all | bytes 131072 | tf_op jit(solution)/shard_map/all_to_all | solution.py:477
  68.0 0.1 loss.1
  68.1 15.8 %all_to_all.23.got_ref = f32[16,1,128]{2,1,0:T(1,128)S(1)} all-to-all(f32[16,1,128]{2,1,0:T(1,128)S(1)} %loss.1), channel_id=1, replica_groups={{0,4,64,68,128,132,192,196,256,260,320,324,384,388,448,452},{8,12,72,76..., dimensions={0} | all-to-all | bytes 16384 | tf_op jit(solution)/shard_map/all_to_all | solution.py:489
  83.9 0.8 finish.1
Async XLA Ops:
  2.9 32.9 %copy-start.1 = (bf16[1,128,384]{2,1,0:T(8,128)(2,1)S(1)}, bf16[1,128,384]{2,1,0:T(8,128)(2,1)}, u32[]{:S(2)}) copy-start(bf16[1,128,384]{2,1,0:T(8,128)(2,1)} %text_key_ref.1) | copy-start | bytes 294916
  2.9 32.9 %copy-start.2 = (bf16[1,128,384]{2,1,0:T(8,128)(2,1)S(1)}, bf16[1,128,384]{2,1,0:T(8,128)(2,1)}, u32[]{:S(2)}) copy-start(bf16[1,128,384]{2,1,0:T(8,128)(2,1)} %text_value_ref.1) | copy-start | bytes 294916
  2.9 32.9 %copy-start.4 = (bf16[384]{0:T(512)(128)(2,1)S(1)}, bf16[384]{0:T(512)(128)(2,1)}, u32[]{:S(2)}) copy-start(bf16[384]{0:T(512)(128)(2,1)} %gain_ref.1) | copy-start | bytes 2308
  30.4 5.4 %copy-start.3 = (bf16[384]{0:T(512)(128)(2,1)S(1)}, bf16[384]{0:T(512)(128)(2,1)}, u32[]{:S(2)}) copy-start(bf16[384]{0:T(512)(128)(2,1)} %mask_ref.1) | copy-start | bytes 2308
  30.4 6.7 %collective-permute-start = (bf16[8,272,128]{2,1,0:T(8,128)(2,1)S(1)}, bf16[8,272,128]{2,1,0:T(8,128)(2,1)S(1)}, u32[]{:S(2)}, u32[]{:S(2)}) collective-permute-start(bf16[8,272,128]{2,1,0:T(8,128)(2,1)S(1)} %all_to_all.20.own_ref), channel_id=1, source_target_pairs={{0,4},{4,0},{8,12},{12,8},{16,20},{20,16},{24,28},{28,24},{32,36},... | collective-permute-start | bytes 1671176 | tf_op jit(solution)/shard_map/ppermute | solution.py:410
  42.6 12.0 %copy-start = (bf16[1,128,384]{2,1,0:T(8,128)(2,1)S(1)}, bf16[1,128,384]{2,1,0:T(8,128)(2,1)}, u32[]{:S(2)}) copy-start(bf16[1,128,384]{2,1,0:T(8,128)(2,1)} %target_ref.1) | copy-start | bytes 294916

commit v4 on v3

--- a/solution.py
+++ b/solution.py
@@ -62,17 +62,20 @@
     place = jnp.where(kept > 0.5, kept_slot, jnp.sum(kept, axis=1, keepdims=True) + rank)
     order = jnp.where(row.astype(jnp.float32) == place, 1.0, 0.0).astype(jnp.bfloat16)
 
-    for copy in copies[1:]:
-        copy.wait()
     scale = HEAD_DIM ** (-0.5)
     match_live = match_live.astype(jnp.bfloat16)
     match_fill = match_fill.astype(jnp.bfloat16)
+    copies[1].wait()
     query = one_hot_dot(match_live, eq_ref[0]) * scale
     dead = jnp.where(live, 0.0, DEAD)
     query = query + jnp.concatenate([dead] * (cols // tokens), axis=1)
+    copies[2].wait()
     key = one_hot_dot(match_fill, ek_ref[0])
+    copies[3].wait()
     value = one_hot_dot(match_live, ev_ref[0])
+    copies[5].wait()
     dec_key = one_hot_dot(order, dk_ref[0])
+    copies[4].wait()
     dec_query = dq_ref[0].astype(jnp.float32) * scale
 
     def low(block, head):
@@ -299,28 +302,28 @@
         return (lambda: query_ref[span, :], key_refs, value_refs, before, use)
 
     dec_group = 2
-    dec_rows = dec_group * tokens
     half = tokens // 2
 
-    def decode(tile):
+    def decode(block, count):
         def use(top, sums):
             found = sums / pltpu.roll(sums, HEAD_DIM, 1)
-            for inner in range(dec_group):
+            for inner in range(count):
                 first = inner * tokens
-                out_ref[tile * dec_group + inner] = jnp.where(
+                out_ref[block + inner] = jnp.where(
                     lane_of(half) < HEAD_DIM,
                     found[first : first + half],
                     pltpu.roll(found[first + half : first + tokens], HEAD_DIM, 1),
                 ).astype(jnp.bfloat16)
 
-        span = slice(tile * dec_rows, (tile + 1) * dec_rows)
+        span = slice(block * tokens, (block + count) * tokens)
         return (lambda: dq_ref[span, :], [dk_ref, pair_dk_ref], [dv_ref], None, use)
 
     jobs = [encode(tile, eq_ref, 0, [pair_ek_ref], [pair_ev_ref], True) for tile in range(2)]
     jobs += [
         encode(tile, pair_eq_ref, chips, [ek_ref, pair_ek_ref], [ev_ref, pair_ev_ref], False) for tile in range(2)
     ]
-    jobs += [decode(tile) for tile in range(chips // dec_group)]
+    jobs += [decode(block, dec_group) for block in range(0, chips - dec_group, dec_group)]
+    jobs += [decode(block, 1) for block in range(chips - dec_group, chips)]
     run_jobs(jobs, (places[0:2], places[2:4]))
 
 
@@ -362,13 +365,21 @@
     loss_ref[...] = jnp.broadcast_to(jnp.sum(total, axis=1, keepdims=True)[None], loss_ref.shape)
 
 
-def finish_kernel(heads, count, att_ref, gain_ref, sums_ref, got_ref, out_ref, loss_ref):
+def finish_kernel(heads, count, att_ref, gain_ref, sums_ref, got_ref, out_ref, loss_ref, done_ref, sems):
     tokens, cols = att_ref.shape
-    loss_ref[...] = (jnp.sum(got_ref[...], axis=0) / count)[0:1, 0:1]
     own = jnp.sum(sums_ref[pl.ds(lax.axis_index("seq") // 2 * heads, heads)], axis=0)
     factor = lax.rsqrt(own[0:1, :] / (cols * heads) + 1e-06)
     column = jnp.transpose(jnp.broadcast_to(factor, (tokens, tokens)))[:, 0:1]
-    out_ref[0] = (att_ref[...] * column * gain_ref[0:1, :]).astype(jnp.bfloat16)
+    half = tokens // 2
+    copies = []
+    for part in range(2):
+        span = slice(part * half, (part + 1) * half)
+        done_ref[span, :] = (att_ref[span, :] * column[span] * gain_ref[0:1, :]).astype(jnp.bfloat16)
+        copies.append(pltpu.make_async_copy(done_ref.at[span], out_ref.at[0, span], sems.at[part]))
+        copies[-1].start()
+    loss_ref[...] = (jnp.sum(got_ref[...], axis=0) / count)[0:1, 0:1]
+    for copy in copies:
+        copy.wait()
 
 
 def local(
@@ -494,7 +505,8 @@
             jax.ShapeDtypeStruct((1, 1), f32),
         ),
         in_specs=vmem(4),
-        out_specs=tuple(vmem(2)),
+        out_specs=(pl.BlockSpec(memory_space=pltpu.HBM), pl.BlockSpec(memory_space=pltpu.VMEM)),
+        scratch_shapes=[pltpu.VMEM((tokens, cols), bf16), pltpu.SemaphoreType.DMA((2,))],
         compiler_params=params(),
         name="finish",
     )(att, gain, sums, got)

time: 85.1 us -> 86.1 us (1.012)
  Pallas kernels: 10.2 us -> 11.2 us
where the time goes in v4:
time: 86.1 us; the launch traced here: 85.7 us
  blocking collectives  68.4 us (79%)
  Pallas kernels  11.2 us (13%)
  starting transfers between devices  4.7 us (5%)
  between operations  1.37 us (2%)
    all_to_all x1, blocking collectives, local(): lax.all_to_all(send, 'seq', 0, 0, axis_index_groups=same_core, tiled=True)  27.5 us
    all_to_all x1, blocking collectives, local(): lax.all_to_all(loss, ('dp', 'seq'), 0, 0, axis_index_groups=columns, tile...  15.8 us
    all_to_all x1, blocking collectives, local(): lax.all_to_all(sums, ('seq', 'head'), 0, 0, axis_index_groups=planes, til...  13.1 us
    all_to_all x1, blocking collectives, local(): lax.all_to_all(out, 'seq', 0, 0, axis_index_groups=same_core, tiled=True)  12 us
    pallas_call x1, Pallas kernels, local(): pl.pallas_call(functools.partial(attend_kernel, slots, tokens), out_shape...  5.64 us
    ppermute x1, starting transfers between devices, local(): lax.ppermute(own, 'seq', [(source, source ^ 1) for source in range(seq)])  4.7 us
    pallas_call x1, Pallas kernels, local(): pl.pallas_call(pack_kernel, out_shape=jax.ShapeDtypeStruct((chips, packed...  2.61 us
  transfers between devices with their start and end apart: 1, of which 0 were waited for; matrix products, arithmetic and copies ran while one was open for 0% of the time, Pallas kernels for 1%

profile of v4, /device:TPU:1, one launch (start us, length us, event | category | flops | bytes accessed | tf_op | source)
XLA Modules:
  0.0 85.7 jit_solution(14362357285263400018)
XLA Ops:
  0.6 2.6 %pack.1 = bf16[8,272,128]{2,1,0:T(8,128)(2,1)} custom-call(s32[1,96]{1,0:T(1,128)} %index_hbm.1, bf16[1,128,384]{2,1,0:T(8,128)(2,1)} %eq_hbm.1, bf16[1,128,384]{2,1,0:T(8,128)(2,1)} %ek_hbm.1, bf16[1,128,384]{2,1,0:T(8,128)(2,1)} %ev_hbm.1, bf16[1,128,384]{2,1,0:T(8,128)(2,1)} %dq_hbm.1, bf16[1,128,384]{2,1,0:T(8,128)(2,1)} %dk_hbm.1), custom_call_target="tpu_custom_call" | custom-call | tf_op jit(solution)/shard_map/pack/pallas_call | solution.py:409
  3.2 0.0 copy-start.1
  3.3 0.0 copy-start.2
  3.3 0.0 copy-start.4
  3.3 27.5 %all_to_all.20.own_ref = bf16[8,272,128]{2,1,0:T(8,128)(2,1)S(1)} all-to-all(bf16[8,272,128]{2,1,0:T(8,128)(2,1)} %pack.1), channel_id=1, replica_groups={{0,8,16,24,32,40,48,56},{4,12,20,28,36,44,52,60},{1,9,17,25,33,41,49,57..., dimensions={0} | all-to-all | bytes 1114112 | tf_op jit(solution)/shard_map/all_to_all | solution.py:420
  30.8 0.0 copy-start.3
  30.8 4.7 %collective-permute-start = (bf16[8,272,128]{2,1,0:T(8,128)(2,1)S(1)}, bf16[8,272,128]{2,1,0:T(8,128)(2,1)S(1)}, u32[]{:S(2)}, u32[]{:S(2)}) collective-permute-start(bf16[8,272,128]{2,1,0:T(8,128)(2,1)S(1)} %all_to_all.20.own_ref), channel_id=1, source_target_pairs={{0,4},{4,0},{8,12},{12,8},{16,20},{20,16},{24,28},{28,24},{32,36},... | collective-permute-start | bytes 1671176 | tf_op jit(solution)/shard_map/ppermute | solution.py:421
  36.1 0.0 copy-done.1
  36.1 0.0 copy-done.2
  36.1 0.0 copy-done.4
  36.2 0.0 copy-done.3
  36.2 1.3 %begin.1 = (bf16[896,128]{1,0:T(8,128)(2,1)S(1)}, bf16[896,128]{1,0:T(8,128)(2,1)S(1)}, bf16[768,128]{1,0:T(8,128)(2,1)S(1)}, bf16[1152,128]{1,0:T(8,128)(2,1)S(...) custom-call(bf16[8,272,128]{2,1,0:T(8,128)(2,1)S(1)} %all_to_all.20., ...), custom_call_target="tpu_custom_call" | custom-call | flops 352321536 | bytes 8388608 | tf_op jit(solution)/shard_map/begin/pallas_call | solution.py:424
  37.4 0.0 collective-permute-done.pair_ref
  37.4 5.6 %attend.1 = bf16[8,64,128]{2,1,0:T(8,128)(2,1)S(1)} custom-call(bf16[8,272,128]{2,1,0:T(8,128)(2,1)S(1)} %collective-permute-done.pair_ref, bf16[896,128]{1,0:T(8,128)(2,1)S(1)} %get-tuple-element.16.ek_ref, bf16[896,128]{1,0:T(8,128)(2,1)S(1)} %get-tuple-element.17.ev_ref, bf16[768,128]{1,0:T(8,128)(2,1)S(1)} %get-tuple-element.18.eq_ref, ...), custom_call_target="tpu_custom_call" | custom-call | tf_op jit(solution)/shard_map/attend/pallas_call | solution.py:453
  43.1 0.0 copy-start
  43.1 12.0 %all_to_all.21.got_ref = bf16[8,64,128]{2,1,0:T(8,128)(2,1)S(1)} all-to-all(bf16[8,64,128]{2,1,0:T(8,128)(2,1)S(1)} %attend.1), channel_id=1, replica_groups={{0,8,16,24,32,40,48,56},{4,12,20,28,36,44,52,60},{1,9,17,25,33,41,49,57..., dimensions={0} | all-to-all | bytes 262144 | tf_op jit(solution)/shard_map/all_to_all | solution.py:473
  55.1 0.0 copy-done
  55.1 0.3 sums.1
  55.4 13.1 %all_to_all.22.sums_ref = f32[32,4,128]{2,1,0:T(4,128)S(1)} all-to-all(f32[32,4,128]{2,1,0:T(4,128)S(1)} %get-tuple-element.27), channel_id=1, replica_groups={{0,1,2,3,8,9,10,11,16,17,18,19,24,25,26,27,32,33,34,35,40,41,42,43,48,4..., dimensions={0} | all-to-all | bytes 131072 | tf_op jit(solution)/shard_map/all_to_all | solution.py:488
  68.5 0.1 loss.1
  68.6 15.8 %all_to_all.23.got_ref = f32[16,1,128]{2,1,0:T(1,128)S(1)} all-to-all(f32[16,1,128]{2,1,0:T(1,128)S(1)} %loss.1), channel_id=1, replica_groups={{0,4,64,68,128,132,192,196,256,260,320,324,384,388,448,452},{8,12,72,76..., dimensions={0} | all-to-all | bytes 16384 | tf_op jit(solution)/shard_map/all_to_all | solution.py:500
  84.4 1.3 %finish.1 = (bf16[1,128,384]{2,1,0:T(8,128)(2,1)}, f32[1,1]{1,0:T(1,128)}) custom-call(f32[128,384]{1,0:T(8,128)S(1)} %get-tuple-element.26.att_ref, f32[8,384]{1,0:T(8,128)S(1)} %get-tuple-element.24.gain_ref, f32[32,4,128]{2,1,0:T(4,128)S(1)} %all_to_all.22.sums_ref, f32[16,1,128]{2,1,0:T(1,128)S(1)} %all_to_all.23.got_ref), custom_call_target="tpu_custom_call" | custom-call | tf_op jit(solution)/shard_map/finish/pallas_call | solution.py:501
Async XLA Ops:
  3.2 32.9 %copy-start.1 = (bf16[1,128,384]{2,1,0:T(8,128)(2,1)S(1)}, bf16[1,128,384]{2,1,0:T(8,128)(2,1)}, u32[]{:S(2)}) copy-start(bf16[1,128,384]{2,1,0:T(8,128)(2,1)} %text_key_ref.1) | copy-start | bytes 294916
  3.3 32.9 %copy-start.2 = (bf16[1,128,384]{2,1,0:T(8,128)(2,1)S(1)}, bf16[1,128,384]{2,1,0:T(8,128)(2,1)}, u32[]{:S(2)}) copy-start(bf16[1,128,384]{2,1,0:T(8,128)(2,1)} %text_value_ref.1) | copy-start | bytes 294916
  3.3 32.9 %copy-start.4 = (bf16[384]{0:T(512)(128)(2,1)S(1)}, bf16[384]{0:T(512)(128)(2,1)}, u32[]{:S(2)}) copy-start(bf16[384]{0:T(512)(128)(2,1)} %gain_ref.1) | copy-start | bytes 2308
  30.8 5.4 %copy-start.3 = (bf16[384]{0:T(512)(128)(2,1)S(1)}, bf16[384]{0:T(512)(128)(2,1)}, u32[]{:S(2)}) copy-start(bf16[384]{0:T(512)(128)(2,1)} %mask_ref.1) | copy-start | bytes 2308
  30.8 6.7 %collective-permute-start = (bf16[8,272,128]{2,1,0:T(8,128)(2,1)S(1)}, bf16[8,272,128]{2,1,0:T(8,128)(2,1)S(1)}, u32[]{:S(2)}, u32[]{:S(2)}) collective-permute-start(bf16[8,272,128]{2,1,0:T(8,128)(2,1)S(1)} %all_to_all.20.own_ref), channel_id=1, source_target_pairs={{0,4},{4,0},{8,12},{12,8},{16,20},{20,16},{24,28},{28,24},{32,36},... | collective-permute-start | bytes 1671176 | tf_op jit(solution)/shard_map/ppermute | solution.py:421
  43.1 12.0 %copy-start = (bf16[1,128,384]{2,1,0:T(8,128)(2,1)S(1)}, bf16[1,128,384]{2,1,0:T(8,128)(2,1)}, u32[]{:S(2)}) copy-start(bf16[1,128,384]{2,1,0:T(8,128)(2,1)} %target_ref.1) | copy-start | bytes 294916

commit v5 on v3

--- a/solution.py
+++ b/solution.py
@@ -28,19 +28,7 @@
     )
 
 
-def pack_kernel(
-    index_hbm, eq_hbm, ek_hbm, ev_hbm, dq_hbm, dk_hbm, send_ref, *scratch
-):
-    *held, sems = scratch
-    given = (index_hbm, eq_hbm, ek_hbm, ev_hbm, dq_hbm, dk_hbm)
-    copies = [
-        pltpu.make_async_copy(source, place, sems.at[number])
-        for number, (source, place) in enumerate(zip(given, held))
-    ]
-    for copy in copies:
-        copy.start()
-    copies[0].wait()
-    index_ref, eq_ref, ek_ref, ev_ref, dq_ref, dk_ref = held
+def pack_kernel(index_ref, eq_ref, ek_ref, ev_ref, dq_ref, dk_ref, send_ref):
     tokens, cols = eq_ref.shape[1:]
     slots = index_ref.shape[1]
     heads = cols // HEAD_DIM
@@ -62,8 +50,6 @@
     place = jnp.where(kept > 0.5, kept_slot, jnp.sum(kept, axis=1, keepdims=True) + rank)
     order = jnp.where(row.astype(jnp.float32) == place, 1.0, 0.0).astype(jnp.bfloat16)
 
-    for copy in copies[1:]:
-        copy.wait()
     scale = HEAD_DIM ** (-0.5)
     match_live = match_live.astype(jnp.bfloat16)
     match_fill = match_fill.astype(jnp.bfloat16)
@@ -398,11 +384,8 @@
     send = pl.pallas_call(
         pack_kernel,
         out_shape=jax.ShapeDtypeStruct((chips, packed, LANES), bf16),
-        in_specs=[pl.BlockSpec(memory_space=pltpu.HBM)] * 6,
+        in_specs=vmem(6),
         out_specs=vmem(1)[0],
-        scratch_shapes=[pltpu.VMEM((1, slots), jnp.int32)]
-        + [pltpu.VMEM((1, tokens, cols), bf16)] * 5
-        + [pltpu.SemaphoreType.DMA((6,))],
         compiler_params=params(60),
         name="pack",
     )(keep_index, enc_query, enc_key, enc_value, dec_query, dec_key)

time: 85.1 us -> 85.2 us (level)
  no operation moved by 1% of the time
where the time goes in v5:
time: 85.2 us; the launch traced here: 84.8 us
  blocking collectives  68.4 us (80%)
  Pallas kernels  10.3 us (12%)
  starting transfers between devices  4.71 us (6%)
  between operations  1.35 us (2%)
    all_to_all x1, blocking collectives, local(): lax.all_to_all(send, 'seq', 0, 0, axis_index_groups=same_core, tiled=True)  27.5 us
    all_to_all x1, blocking collectives, local(): lax.all_to_all(loss, ('dp', 'seq'), 0, 0, axis_index_groups=columns, tile...  15.8 us
    all_to_all x1, blocking collectives, local(): lax.all_to_all(sums, ('seq', 'head'), 0, 0, axis_index_groups=planes, til...  13.1 us
    all_to_all x1, blocking collectives, local(): lax.all_to_all(out, 'seq', 0, 0, axis_index_groups=same_core, tiled=True)  12 us
    pallas_call x1, Pallas kernels, local(): pl.pallas_call(functools.partial(attend_kernel, slots, tokens), out_shape...  5.46 us
    ppermute x1, starting transfers between devices, local(): lax.ppermute(own, 'seq', [(source, source ^ 1) for source in range(seq)])  4.71 us
    pallas_call x1, Pallas kernels, local(): pl.pallas_call(pack_kernel, out_shape=jax.ShapeDtypeStruct((chips, packed...  2.36 us
  transfers between devices with their start and end apart: 1, of which 0 were waited for; matrix products, arithmetic and copies ran while one was open for 0% of the time, Pallas kernels for 1%

profile of v5, /device:TPU:1, one launch (start us, length us, event | category | flops | bytes accessed | tf_op | source)
XLA Modules:
  0.0 84.8 jit_solution(14341909731840130195)
XLA Ops:
  0.6 2.4 %pack.1 = bf16[8,272,128]{2,1,0:T(8,128)(2,1)} custom-call(s32[1,96]{1,0:T(1,128)} %index_ref.1, bf16[1,128,384]{2,1,0:T(8,128)(2,1)} %eq_ref.1, bf16[1,128,384]{2,1,0:T(8,128)(2,1)} %ek_ref.1, bf16[1,128,384]{2,1,0:T(8,128)(2,1)} %ev_ref.1, bf16[1,128,384]{2,1,0:T(8,128)(2,1)} %dq_ref.1, bf16[1,128,384]{2,1,0:T(8,128)(2,1)} %dk_ref.1), custom_call_target="tpu_custom_call" | custom-call | tf_op jit(solution)/shard_map/pack/pallas_call | solution.py:384
  3.0 0.0 copy-start.1
  3.0 0.0 copy-start.2
  3.0 0.0 copy-start.4
  3.0 27.5 %all_to_all.20.own_ref = bf16[8,272,128]{2,1,0:T(8,128)(2,1)S(1)} all-to-all(bf16[8,272,128]{2,1,0:T(8,128)(2,1)} %pack.1), channel_id=1, replica_groups={{0,8,16,24,32,40,48,56},{4,12,20,28,36,44,52,60},{1,9,17,25,33,41,49,57..., dimensions={0} | all-to-all | bytes 1114112 | tf_op jit(solution)/shard_map/all_to_all | solution.py:392
  30.5 0.0 copy-start.3
  30.5 4.7 %collective-permute-start = (bf16[8,272,128]{2,1,0:T(8,128)(2,1)S(1)}, bf16[8,272,128]{2,1,0:T(8,128)(2,1)S(1)}, u32[]{:S(2)}, u32[]{:S(2)}) collective-permute-start(bf16[8,272,128]{2,1,0:T(8,128)(2,1)S(1)} %all_to_all.20.own_ref), channel_id=1, source_target_pairs={{0,4},{4,0},{8,12},{12,8},{16,20},{20,16},{24,28},{28,24},{32,36},... | collective-permute-start | bytes 1671176 | tf_op jit(solution)/shard_map/ppermute | solution.py:393
  35.8 0.0 copy-done.1
  35.9 0.0 copy-done.2
  35.9 0.0 copy-done.4
  35.9 0.0 copy-done.3
  35.9 1.3 %begin.1 = (bf16[896,128]{1,0:T(8,128)(2,1)S(1)}, bf16[896,128]{1,0:T(8,128)(2,1)S(1)}, bf16[768,128]{1,0:T(8,128)(2,1)S(1)}, bf16[1152,128]{1,0:T(8,128)(2,1)S(...) custom-call(bf16[8,272,128]{2,1,0:T(8,128)(2,1)S(1)} %all_to_all.20., ...), custom_call_target="tpu_custom_call" | custom-call | flops 352321536 | bytes 8388608 | tf_op jit(solution)/shard_map/begin/pallas_call | solution.py:396
  37.2 0.0 collective-permute-done.pair_ref
  37.2 5.5 %attend.1 = bf16[8,64,128]{2,1,0:T(8,128)(2,1)S(1)} custom-call(bf16[8,272,128]{2,1,0:T(8,128)(2,1)S(1)} %collective-permute-done.pair_ref, bf16[896,128]{1,0:T(8,128)(2,1)S(1)} %get-tuple-element.16.ek_ref, bf16[896,128]{1,0:T(8,128)(2,1)S(1)} %get-tuple-element.17.ev_ref, bf16[768,128]{1,0:T(8,128)(2,1)S(1)} %get-tuple-element.18.eq_ref, ...), custom_call_target="tpu_custom_call" | custom-call | tf_op jit(solution)/shard_map/attend/pallas_call | solution.py:425
  42.6 0.0 copy-start
  42.6 12.0 %all_to_all.21.got_ref = bf16[8,64,128]{2,1,0:T(8,128)(2,1)S(1)} all-to-all(bf16[8,64,128]{2,1,0:T(8,128)(2,1)S(1)} %attend.1), channel_id=1, replica_groups={{0,8,16,24,32,40,48,56},{4,12,20,28,36,44,52,60},{1,9,17,25,33,41,49,57..., dimensions={0} | all-to-all | bytes 262144 | tf_op jit(solution)/shard_map/all_to_all | solution.py:445
  54.6 0.0 copy-done
  54.6 0.3 sums.1
  54.9 13.1 %all_to_all.22.sums_ref = f32[32,4,128]{2,1,0:T(4,128)S(1)} all-to-all(f32[32,4,128]{2,1,0:T(4,128)S(1)} %get-tuple-element.27), channel_id=1, replica_groups={{0,1,2,3,8,9,10,11,16,17,18,19,24,25,26,27,32,33,34,35,40,41,42,43,48,4..., dimensions={0} | all-to-all | bytes 131072 | tf_op jit(solution)/shard_map/all_to_all | solution.py:460
  68.0 0.1 loss.1
  68.1 15.8 %all_to_all.23.got_ref = f32[16,1,128]{2,1,0:T(1,128)S(1)} all-to-all(f32[16,1,128]{2,1,0:T(1,128)S(1)} %loss.1), channel_id=1, replica_groups={{0,4,64,68,128,132,192,196,256,260,320,324,384,388,448,452},{8,12,72,76..., dimensions={0} | all-to-all | bytes 16384 | tf_op jit(solution)/shard_map/all_to_all | solution.py:472
  83.9 0.8 finish.1
Async XLA Ops:
  3.0 32.9 %copy-start.1 = (bf16[1,128,384]{2,1,0:T(8,128)(2,1)S(1)}, bf16[1,128,384]{2,1,0:T(8,128)(2,1)}, u32[]{:S(2)}) copy-start(bf16[1,128,384]{2,1,0:T(8,128)(2,1)} %text_key_ref.1) | copy-start | bytes 294916
  3.0 32.9 %copy-start.2 = (bf16[1,128,384]{2,1,0:T(8,128)(2,1)S(1)}, bf16[1,128,384]{2,1,0:T(8,128)(2,1)}, u32[]{:S(2)}) copy-start(bf16[1,128,384]{2,1,0:T(8,128)(2,1)} %text_value_ref.1) | copy-start | bytes 294916
  3.0 32.9 %copy-start.4 = (bf16[384]{0:T(512)(128)(2,1)S(1)}, bf16[384]{0:T(512)(128)(2,1)}, u32[]{:S(2)}) copy-start(bf16[384]{0:T(512)(128)(2,1)} %gain_ref.1) | copy-start | bytes 2308
  30.5 5.4 %copy-start.3 = (bf16[384]{0:T(512)(128)(2,1)S(1)}, bf16[384]{0:T(512)(128)(2,1)}, u32[]{:S(2)}) copy-start(bf16[384]{0:T(512)(128)(2,1)} %mask_ref.1) | copy-start | bytes 2308
  30.5 6.7 %collective-permute-start = (bf16[8,272,128]{2,1,0:T(8,128)(2,1)S(1)}, bf16[8,272,128]{2,1,0:T(8,128)(2,1)S(1)}, u32[]{:S(2)}, u32[]{:S(2)}) collective-permute-start(bf16[8,272,128]{2,1,0:T(8,128)(2,1)S(1)} %all_to_all.20.own_ref), channel_id=1, source_target_pairs={{0,4},{4,0},{8,12},{12,8},{16,20},{20,16},{24,28},{28,24},{32,36},... | collective-permute-start | bytes 1671176 | tf_op jit(solution)/shard_map/ppermute | solution.py:393
  42.6 12.0 %copy-start = (bf16[1,128,384]{2,1,0:T(8,128)(2,1)S(1)}, bf16[1,128,384]{2,1,0:T(8,128)(2,1)}, u32[]{:S(2)}) copy-start(bf16[1,128,384]{2,1,0:T(8,128)(2,1)} %target_ref.1) | copy-start | bytes 294916

commit v6 on v3

--- a/solution.py
+++ b/solution.py
@@ -365,10 +365,18 @@
 def finish_kernel(heads, count, att_ref, gain_ref, sums_ref, got_ref, out_ref, loss_ref):
     tokens, cols = att_ref.shape
     loss_ref[...] = (jnp.sum(got_ref[...], axis=0) / count)[0:1, 0:1]
-    own = jnp.sum(sums_ref[pl.ds(lax.axis_index("seq") // 2 * heads, heads)], axis=0)
+    half = sums_ref.shape[0] // heads // 2
+    chip = lax.axis_index("seq") // 2
+    listed = 2 * lax.rem(chip, half) + chip // half
+    own = jnp.sum(sums_ref[pl.ds(listed * heads, heads)], axis=0)
     factor = lax.rsqrt(own[0:1, :] / (cols * heads) + 1e-06)
     column = jnp.transpose(jnp.broadcast_to(factor, (tokens, tokens)))[:, 0:1]
     out_ref[0] = (att_ref[...] * column * gain_ref[0:1, :]).astype(jnp.bfloat16)
+
+
+def far_first(count):
+    half = max(count // 2, 1)
+    return [place + side * half for place in range(half) for side in range(count // half)]
 
 
 def local(
@@ -472,7 +480,7 @@
         name="sums",
     )(got, gain, target, weight)
     planes = [
-        [(2 * chip + core) * heads + head for chip in range(chips) for head in range(heads)] for core in range(2)
+        [(2 * chip + core) * heads + head for chip in far_first(chips) for head in range(heads)] for core in range(2)
     ]
     sums = lax.all_to_all(sums, ("seq", "head"), 0, 0, axis_index_groups=planes, tiled=True)
     loss = pl.pallas_call(
@@ -484,7 +492,7 @@
         name="loss",
     )(sums)
     columns = [
-        [image * seq + 2 * chip + core for image in range(images) for core in range(2)] for chip in range(chips)
+        [image * seq + 2 * chip + core for image in far_first(images) for core in range(2)] for chip in range(chips)
     ]
     got = lax.all_to_all(loss, ("dp", "seq"), 0, 0, axis_index_groups=columns, tiled=True)
     decoded, loss = pl.pallas_call(

time: 85.1 us -> 85.4 us (level)
  no operation moved by 1% of the time
where the time goes in v6:
time: 85.4 us; the launch traced here: 85 us
  blocking collectives  68.6 us (80%)
  Pallas kernels  10.2 us (12%)
  starting transfers between devices  4.73 us (6%)
  between operations  1.37 us (2%)
    all_to_all x1, blocking collectives, local(): lax.all_to_all(send, 'seq', 0, 0, axis_index_groups=same_core, tiled=True)  27.5 us
    all_to_all x1, blocking collectives, local(): lax.all_to_all(loss, ('dp', 'seq'), 0, 0, axis_index_groups=columns, tile...  15.9 us
    all_to_all x1, blocking collectives, local(): lax.all_to_all(sums, ('seq', 'head'), 0, 0, axis_index_groups=planes, til...  13.3 us
    all_to_all x1, blocking collectives, local(): lax.all_to_all(out, 'seq', 0, 0, axis_index_groups=same_core, tiled=True)  12 us
    pallas_call x1, Pallas kernels, local(): pl.pallas_call(functools.partial(attend_kernel, slots, tokens), out_shape...  5.45 us
    ppermute x1, starting transfers between devices, local(): lax.ppermute(own, 'seq', [(source, source ^ 1) for source in range(seq)])  4.73 us
    pallas_call x1, Pallas kernels, local(): pl.pallas_call(pack_kernel, out_shape=jax.ShapeDtypeStruct((chips, packed...  2.29 us
  transfers between devices with their start and end apart: 1, of which 0 were waited for; matrix products, arithmetic and copies ran while one was open for 0% of the time, Pallas kernels for 1%

profile of v6, /device:TPU:1, one launch (start us, length us, event | category | flops | bytes accessed | tf_op | source)
XLA Modules:
  0.0 85.0 jit_solution(15201221306033413762)
XLA Ops:
  0.6 2.3 %pack.1 = bf16[8,272,128]{2,1,0:T(8,128)(2,1)} custom-call(s32[1,96]{1,0:T(1,128)} %index_hbm.1, bf16[1,128,384]{2,1,0:T(8,128)(2,1)} %eq_hbm.1, bf16[1,128,384]{2,1,0:T(8,128)(2,1)} %ek_hbm.1, bf16[1,128,384]{2,1,0:T(8,128)(2,1)} %ev_hbm.1, bf16[1,128,384]{2,1,0:T(8,128)(2,1)} %dq_hbm.1, bf16[1,128,384]{2,1,0:T(8,128)(2,1)} %dk_hbm.1), custom_call_target="tpu_custom_call" | custom-call | tf_op jit(solution)/shard_map/pack/pallas_call | solution.py:406
  2.9 0.0 copy-start.1
  2.9 0.0 copy-start.2
  2.9 0.0 copy-start.4
  3.0 27.5 %all_to_all.20.own_ref = bf16[8,272,128]{2,1,0:T(8,128)(2,1)S(1)} all-to-all(bf16[8,272,128]{2,1,0:T(8,128)(2,1)} %pack.1), channel_id=1, replica_groups={{0,8,16,24,32,40,48,56},{4,12,20,28,36,44,52,60},{1,9,17,25,33,41,49,57..., dimensions={0} | all-to-all | bytes 1114112 | tf_op jit(solution)/shard_map/all_to_all | solution.py:417
  30.4 0.0 copy-start.3
  30.4 4.7 %collective-permute-start = (bf16[8,272,128]{2,1,0:T(8,128)(2,1)S(1)}, bf16[8,272,128]{2,1,0:T(8,128)(2,1)S(1)}, u32[]{:S(2)}, u32[]{:S(2)}) collective-permute-start(bf16[8,272,128]{2,1,0:T(8,128)(2,1)S(1)} %all_to_all.20.own_ref), channel_id=1, source_target_pairs={{0,4},{4,0},{8,12},{12,8},{16,20},{20,16},{24,28},{28,24},{32,36},... | collective-permute-start | bytes 1671176 | tf_op jit(solution)/shard_map/ppermute | solution.py:418
  35.8 0.0 copy-done.1
  35.8 0.0 copy-done.2
  35.8 0.0 copy-done.4
  35.8 0.0 copy-done.3
  35.8 1.3 %begin.1 = (bf16[896,128]{1,0:T(8,128)(2,1)S(1)}, bf16[896,128]{1,0:T(8,128)(2,1)S(1)}, bf16[768,128]{1,0:T(8,128)(2,1)S(1)}, bf16[1152,128]{1,0:T(8,128)(2,1)S(...) custom-call(bf16[8,272,128]{2,1,0:T(8,128)(2,1)S(1)} %all_to_all.20., ...), custom_call_target="tpu_custom_call" | custom-call | flops 352321536 | bytes 8388608 | tf_op jit(solution)/shard_map/begin/pallas_call | solution.py:421
  37.1 0.0 collective-permute-done.pair_ref
  37.1 5.5 %attend.1 = bf16[8,64,128]{2,1,0:T(8,128)(2,1)S(1)} custom-call(bf16[8,272,128]{2,1,0:T(8,128)(2,1)S(1)} %collective-permute-done.pair_ref, bf16[896,128]{1,0:T(8,128)(2,1)S(1)} %get-tuple-element.16.ek_ref, bf16[896,128]{1,0:T(8,128)(2,1)S(1)} %get-tuple-element.17.ev_ref, bf16[768,128]{1,0:T(8,128)(2,1)S(1)} %get-tuple-element.18.eq_ref, ...), custom_call_target="tpu_custom_call" | custom-call | tf_op jit(solution)/shard_map/attend/pallas_call | solution.py:450
  42.6 0.0 copy-start
  42.6 12.0 %all_to_all.21.got_ref = bf16[8,64,128]{2,1,0:T(8,128)(2,1)S(1)} all-to-all(bf16[8,64,128]{2,1,0:T(8,128)(2,1)S(1)} %attend.1), channel_id=1, replica_groups={{0,8,16,24,32,40,48,56},{4,12,20,28,36,44,52,60},{1,9,17,25,33,41,49,57..., dimensions={0} | all-to-all | bytes 262144 | tf_op jit(solution)/shard_map/all_to_all | solution.py:470
  54.6 0.0 copy-done
  54.6 0.3 sums.1
  54.9 13.3 %all_to_all.22.sums_ref = f32[32,4,128]{2,1,0:T(4,128)S(1)} all-to-all(f32[32,4,128]{2,1,0:T(4,128)S(1)} %get-tuple-element.27), channel_id=1, replica_groups={{0,1,2,3,32,33,34,35,8,9,10,11,40,41,42,43,16,17,18,19,48,49,50,51,24,2..., dimensions={0} | all-to-all | bytes 131072 | tf_op jit(solution)/shard_map/all_to_all | solution.py:485
  68.2 0.1 loss.1
  68.3 15.9 %all_to_all.23.got_ref = f32[16,1,128]{2,1,0:T(1,128)S(1)} all-to-all(f32[16,1,128]{2,1,0:T(1,128)S(1)} %loss.1), channel_id=1, replica_groups={{0,4,256,260,64,68,320,324,128,132,384,388,192,196,448,452},{8,12,264,2..., dimensions={0} | all-to-all | bytes 16384 | tf_op jit(solution)/shard_map/all_to_all | solution.py:497
  84.2 0.8 finish.1
Async XLA Ops:
  2.9 32.9 %copy-start.1 = (bf16[1,128,384]{2,1,0:T(8,128)(2,1)S(1)}, bf16[1,128,384]{2,1,0:T(8,128)(2,1)}, u32[]{:S(2)}) copy-start(bf16[1,128,384]{2,1,0:T(8,128)(2,1)} %text_key_ref.1) | copy-start | bytes 294916
  2.9 32.9 %copy-start.2 = (bf16[1,128,384]{2,1,0:T(8,128)(2,1)S(1)}, bf16[1,128,384]{2,1,0:T(8,128)(2,1)}, u32[]{:S(2)}) copy-start(bf16[1,128,384]{2,1,0:T(8,128)(2,1)} %text_value_ref.1) | copy-start | bytes 294916
  2.9 32.9 %copy-start.4 = (bf16[384]{0:T(512)(128)(2,1)S(1)}, bf16[384]{0:T(512)(128)(2,1)}, u32[]{:S(2)}) copy-start(bf16[384]{0:T(512)(128)(2,1)} %gain_ref.1) | copy-start | bytes 2308
  30.4 5.4 %copy-start.3 = (bf16[384]{0:T(512)(128)(2,1)S(1)}, bf16[384]{0:T(512)(128)(2,1)}, u32[]{:S(2)}) copy-start(bf16[384]{0:T(512)(128)(2,1)} %mask_ref.1) | copy-start | bytes 2308
  30.4 6.7 %collective-permute-start = (bf16[8,272,128]{2,1,0:T(8,128)(2,1)S(1)}, bf16[8,272,128]{2,1,0:T(8,128)(2,1)S(1)}, u32[]{:S(2)}, u32[]{:S(2)}) collective-permute-start(bf16[8,272,128]{2,1,0:T(8,128)(2,1)S(1)} %all_to_all.20.own_ref), channel_id=1, source_target_pairs={{0,4},{4,0},{8,12},{12,8},{16,20},{20,16},{24,28},{28,24},{32,36},... | collective-permute-start | bytes 1671176 | tf_op jit(solution)/shard_map/ppermute | solution.py:418
  42.6 12.0 %copy-start = (bf16[1,128,384]{2,1,0:T(8,128)(2,1)S(1)}, bf16[1,128,384]{2,1,0:T(8,128)(2,1)}, u32[]{:S(2)}) copy-start(bf16[1,128,384]{2,1,0:T(8,128)(2,1)} %target_ref.1) | copy-start | bytes 294916

commit v7 on v3

--- a/solution.py
+++ b/solution.py
@@ -278,10 +278,9 @@
     dv_ref[0:tokens, :] = ev_ref[0:tokens, :]
     mask_row = fill_ref[0:1, :]
     fill = jnp.broadcast_to(mask_row, (spare, LANES)).astype(jnp.bfloat16)
-    group = chips // 2
-    rows = group * slots
-
-    def encode(tile, query_ref, first_block, key_refs, value_refs, earlier):
+
+    def encode(tile, group, query_ref, first_block, key_refs, value_refs, earlier):
+        rows = group * slots
         span = slice(tile * rows, (tile + 1) * rows)
 
         def use(top, sums):
@@ -316,9 +315,10 @@
         span = slice(tile * dec_rows, (tile + 1) * dec_rows)
         return (lambda: dq_ref[span, :], [dk_ref, pair_dk_ref], [dv_ref], None, use)
 
-    jobs = [encode(tile, eq_ref, 0, [pair_ek_ref], [pair_ev_ref], True) for tile in range(2)]
+    jobs = [encode(0, chips, eq_ref, 0, [pair_ek_ref], [pair_ev_ref], True)]
     jobs += [
-        encode(tile, pair_eq_ref, chips, [ek_ref, pair_ek_ref], [ev_ref, pair_ev_ref], False) for tile in range(2)
+        encode(tile, chips // 2, pair_eq_ref, chips, [ek_ref, pair_ek_ref], [ev_ref, pair_ev_ref], False)
+        for tile in range(2)
     ]
     jobs += [decode(tile) for tile in range(chips // dec_group)]
     run_jobs(jobs, (places[0:2], places[2:4]))
@@ -452,8 +452,8 @@
             pltpu.VMEM((tokens + 2 * dec_own, LANES), bf16),
         ]
         + [
-            pltpu.VMEM((kept_own // 2, tokens + 2 * dec_own), f32),
-            pltpu.VMEM((kept_own // 2, LANES), f32),
+            pltpu.VMEM((kept_own, tokens + 2 * dec_own), f32),
+            pltpu.VMEM((kept_own, LANES), f32),
         ]
         * 2,
         compiler_params=params(),

time: 85.1 us -> 85.5 us (level)
  no operation moved by 1% of the time
where the time goes in v7:
time: 85.5 us; the launch traced here: 85.1 us
  blocking collectives  68.4 us (80%)
  Pallas kernels  10.6 us (12%)
  starting transfers between devices  4.73 us (6%)
  between operations  1.37 us (2%)
    all_to_all x1, blocking collectives, local(): lax.all_to_all(send, 'seq', 0, 0, axis_index_groups=same_core, tiled=True)  27.5 us
    all_to_all x1, blocking collectives, local(): lax.all_to_all(loss, ('dp', 'seq'), 0, 0, axis_index_groups=columns, tile...  15.8 us
    all_to_all x1, blocking collectives, local(): lax.all_to_all(sums, ('seq', 'head'), 0, 0, axis_index_groups=planes, til...  13.1 us
    all_to_all x1, blocking collectives, local(): lax.all_to_all(out, 'seq', 0, 0, axis_index_groups=same_core, tiled=True)  12 us
    pallas_call x1, Pallas kernels, local(): pl.pallas_call(functools.partial(attend_kernel, slots, tokens), out_shape...  5.84 us
    ppermute x1, starting transfers between devices, local(): lax.ppermute(own, 'seq', [(source, source ^ 1) for source in range(seq)])  4.73 us
    pallas_call x1, Pallas kernels, local(): pl.pallas_call(pack_kernel, out_shape=jax.ShapeDtypeStruct((chips, packed...  2.29 us
  transfers between devices with their start and end apart: 1, of which 0 were waited for; matrix products, arithmetic and copies ran while one was open for 0% of the time, Pallas kernels for 1%

profile of v7, /device:TPU:1, one launch (start us, length us, event | category | flops | bytes accessed | tf_op | source)
XLA Modules:
  0.0 85.1 jit_solution(7918489825405363901)
XLA Ops:
  0.6 2.3 %pack.1 = bf16[8,272,128]{2,1,0:T(8,128)(2,1)} custom-call(s32[1,96]{1,0:T(1,128)} %index_hbm.1, bf16[1,128,384]{2,1,0:T(8,128)(2,1)} %eq_hbm.1, bf16[1,128,384]{2,1,0:T(8,128)(2,1)} %ek_hbm.1, bf16[1,128,384]{2,1,0:T(8,128)(2,1)} %ev_hbm.1, bf16[1,128,384]{2,1,0:T(8,128)(2,1)} %dq_hbm.1, bf16[1,128,384]{2,1,0:T(8,128)(2,1)} %dk_hbm.1), custom_call_target="tpu_custom_call" | custom-call | tf_op jit(solution)/shard_map/pack/pallas_call | solution.py:398
  2.9 0.0 copy-start.1
  2.9 0.0 copy-start.2
  2.9 0.0 copy-start.4
  3.0 27.5 %all_to_all.20.own_ref = bf16[8,272,128]{2,1,0:T(8,128)(2,1)S(1)} all-to-all(bf16[8,272,128]{2,1,0:T(8,128)(2,1)} %pack.1), channel_id=1, replica_groups={{0,8,16,24,32,40,48,56},{4,12,20,28,36,44,52,60},{1,9,17,25,33,41,49,57..., dimensions={0} | all-to-all | bytes 1114112 | tf_op jit(solution)/shard_map/all_to_all | solution.py:409
  30.4 0.0 copy-start.3
  30.4 4.7 %collective-permute-start = (bf16[8,272,128]{2,1,0:T(8,128)(2,1)S(1)}, bf16[8,272,128]{2,1,0:T(8,128)(2,1)S(1)}, u32[]{:S(2)}, u32[]{:S(2)}) collective-permute-start(bf16[8,272,128]{2,1,0:T(8,128)(2,1)S(1)} %all_to_all.20.own_ref), channel_id=1, source_target_pairs={{0,4},{4,0},{8,12},{12,8},{16,20},{20,16},{24,28},{28,24},{32,36},... | collective-permute-start | bytes 1671176 | tf_op jit(solution)/shard_map/ppermute | solution.py:410
  35.8 0.0 copy-done.1
  35.8 0.0 copy-done.2
  35.8 0.0 copy-done.4
  35.8 0.0 copy-done.3
  35.8 1.3 %begin.1 = (bf16[896,128]{1,0:T(8,128)(2,1)S(1)}, bf16[896,128]{1,0:T(8,128)(2,1)S(1)}, bf16[768,128]{1,0:T(8,128)(2,1)S(1)}, bf16[1152,128]{1,0:T(8,128)(2,1)S(...) custom-call(bf16[8,272,128]{2,1,0:T(8,128)(2,1)S(1)} %all_to_all.20., ...), custom_call_target="tpu_custom_call" | custom-call | flops 352321536 | bytes 8388608 | tf_op jit(solution)/shard_map/begin/pallas_call | solution.py:413
  37.1 0.0 collective-permute-done.pair_ref
  37.1 5.8 %attend.1 = bf16[8,64,128]{2,1,0:T(8,128)(2,1)S(1)} custom-call(bf16[8,272,128]{2,1,0:T(8,128)(2,1)S(1)} %collective-permute-done.pair_ref, bf16[896,128]{1,0:T(8,128)(2,1)S(1)} %get-tuple-element.16.ek_ref, bf16[896,128]{1,0:T(8,128)(2,1)S(1)} %get-tuple-element.17.ev_ref, bf16[768,128]{1,0:T(8,128)(2,1)S(1)} %get-tuple-element.18.eq_ref, ...), custom_call_target="tpu_custom_call" | custom-call | tf_op jit(solution)/shard_map/attend/pallas_call | solution.py:442
  43.0 0.0 copy-start
  43.0 12.0 %all_to_all.21.got_ref = bf16[8,64,128]{2,1,0:T(8,128)(2,1)S(1)} all-to-all(bf16[8,64,128]{2,1,0:T(8,128)(2,1)S(1)} %attend.1), channel_id=1, replica_groups={{0,8,16,24,32,40,48,56},{4,12,20,28,36,44,52,60},{1,9,17,25,33,41,49,57..., dimensions={0} | all-to-all | bytes 262144 | tf_op jit(solution)/shard_map/all_to_all | solution.py:462
  55.0 0.0 copy-done
  55.0 0.3 sums.1
  55.2 13.1 %all_to_all.22.sums_ref = f32[32,4,128]{2,1,0:T(4,128)S(1)} all-to-all(f32[32,4,128]{2,1,0:T(4,128)S(1)} %get-tuple-element.27), channel_id=1, replica_groups={{0,1,2,3,8,9,10,11,16,17,18,19,24,25,26,27,32,33,34,35,40,41,42,43,48,4..., dimensions={0} | all-to-all | bytes 131072 | tf_op jit(solution)/shard_map/all_to_all | solution.py:477
  68.4 0.1 loss.1
  68.5 15.8 %all_to_all.23.got_ref = f32[16,1,128]{2,1,0:T(1,128)S(1)} all-to-all(f32[16,1,128]{2,1,0:T(1,128)S(1)} %loss.1), channel_id=1, replica_groups={{0,4,64,68,128,132,192,196,256,260,320,324,384,388,448,452},{8,12,72,76..., dimensions={0} | all-to-all | bytes 16384 | tf_op jit(solution)/shard_map/all_to_all | solution.py:489
  84.3 0.8 finish.1
Async XLA Ops:
  2.9 32.9 %copy-start.1 = (bf16[1,128,384]{2,1,0:T(8,128)(2,1)S(1)}, bf16[1,128,384]{2,1,0:T(8,128)(2,1)}, u32[]{:S(2)}) copy-start(bf16[1,128,384]{2,1,0:T(8,128)(2,1)} %text_key_ref.1) | copy-start | bytes 294916
  2.9 32.9 %copy-start.2 = (bf16[1,128,384]{2,1,0:T(8,128)(2,1)S(1)}, bf16[1,128,384]{2,1,0:T(8,128)(2,1)}, u32[]{:S(2)}) copy-start(bf16[1,128,384]{2,1,0:T(8,128)(2,1)} %text_value_ref.1) | copy-start | bytes 294916
  2.9 32.9 %copy-start.4 = (bf16[384]{0:T(512)(128)(2,1)S(1)}, bf16[384]{0:T(512)(128)(2,1)}, u32[]{:S(2)}) copy-start(bf16[384]{0:T(512)(128)(2,1)} %gain_ref.1) | copy-start | bytes 2308
  30.4 5.4 %copy-start.3 = (bf16[384]{0:T(512)(128)(2,1)S(1)}, bf16[384]{0:T(512)(128)(2,1)}, u32[]{:S(2)}) copy-start(bf16[384]{0:T(512)(128)(2,1)} %mask_ref.1) | copy-start | bytes 2308
  30.4 6.7 %collective-permute-start = (bf16[8,272,128]{2,1,0:T(8,128)(2,1)S(1)}, bf16[8,272,128]{2,1,0:T(8,128)(2,1)S(1)}, u32[]{:S(2)}, u32[]{:S(2)}) collective-permute-start(bf16[8,272,128]{2,1,0:T(8,128)(2,1)S(1)} %all_to_all.20.own_ref), channel_id=1, source_target_pairs={{0,4},{4,0},{8,12},{12,8},{16,20},{20,16},{24,28},{28,24},{32,36},... | collective-permute-start | bytes 1671176 | tf_op jit(solution)/shard_map/ppermute | solution.py:410
  43.0 12.0 %copy-start = (bf16[1,128,384]{2,1,0:T(8,128)(2,1)S(1)}, bf16[1,128,384]{2,1,0:T(8,128)(2,1)}, u32[]{:S(2)}) copy-start(bf16[1,128,384]{2,1,0:T(8,128)(2,1)} %target_ref.1) | copy-start | bytes 294916
